TPU v7x, 768 devices: a whole 4x8x12 slice. The times are simulated.
768 devices in a mesh: outer: 32 (over y_hi, x, core), inner: 24 (over z, y_lo).
Axes of the slice: x: 4, y: 8 (y_hi: 4, y_lo: 2; y = y_hi * 2 + y_lo), z: 12, core: 2. Of those that a mesh axis runs over, the one named last changes fastest.
Arguments:
- images: bfloat16 [12288, 1152], P(('outer', 'inner')), as said below
- texts: bfloat16 [98304, 1152], P(('outer', 'inner')), as said below
- logit_scale: float32 [1], replicated, may hold values from 8 to 20
- logit_bias: float32 [1], replicated, may hold values from -2 to 0
Outputs:
- grad_images: float32 [12288, 1152], P(('outer', 'inner'))
- grad_texts: float32 [98304, 1152], P(('outer', 'inner'))
Inputs may be any that keep to these rules, and one draw needn't show every extreme that they name: `images`: entries are finite. `texts`: entries are finite.
All inputs are finite; a program needn't handle non-finite values.
Results may differ from a plain program's by a relative error of at most 0.002.
Values may be sent and summed in bfloat16 or wider, within the bound.
A program may use at most 32 MiB of HBM per device.

v0:
```python
import math

import jax
import jax.numpy as jnp
from jax import lax
from jax.sharding import PartitionSpec as P

HALF = 3


def shifted(x, axis, by):
    size = lax.axis_size(axis)
    return lax.ppermute(x, axis, [(i, (i + by) % size) for i in range(size)])


def unit_rows(values):
    widened = values.astype(jnp.float32)
    inverse = lax.rsqrt(jnp.sum(widened * widened, axis=-1, keepdims=True) + 1e-06)
    return (inverse, widened * inverse)


def project_back(inverse, unit_full, gradient):
    along = jnp.sum(unit_full * gradient, axis=-1, keepdims=True)
    return inverse * (gradient - unit_full * along)


def local(images, texts, logit_scale, logit_bias):
    outer_count = lax.axis_size("outer")
    inner_count = lax.axis_size("inner")
    my_outer = lax.axis_index("outer")
    my_inner = lax.axis_index("inner")
    img_rows = images.shape[0]
    txt_rows = texts.shape[0]
    factor = logit_scale[0]
    offset = logit_bias[0]
    divisor = 1.0 / math.sqrt((2 * HALF + 1) * inner_count * txt_rows)
    inverse_img, full_img = unit_rows(images)
    inverse_txt, full_txt = unit_rows(texts)
    unit_txt = full_txt.astype(jnp.bfloat16)
    group_imgs = lax.all_gather(full_img.astype(jnp.bfloat16), "inner", axis=0, tiled=True)
    row_ids = jnp.arange(group_imgs.shape[0], dtype=jnp.int32)
    own_block = (row_ids // img_rows == my_inner)[:, None]
    same_slot = (row_ids % img_rows)[:, None] == jnp.arange(txt_rows, dtype=jnp.int32)[None, :]
    diagonal = jnp.logical_and(own_block, same_slot)

    def tile_terms(held_text, anchor):
        logits = (
            jnp.dot(group_imgs, held_text.T, preferred_element_type=jnp.float32) * factor + offset
        )
        matched = jnp.logical_and(diagonal, anchor == my_outer)
        labels = jnp.where(matched, 1.0, -1.0).astype(jnp.float32)
        weights = (-labels * jax.nn.sigmoid(-labels * logits) * divisor).astype(jnp.bfloat16)
        image_part = jnp.dot(weights, held_text, preferred_element_type=jnp.float32) * factor
        text_part = (
            lax.dot_general(
                weights, group_imgs, (((0,), (0,)), ((), ())), preferred_element_type=jnp.float32
            )
            * factor
        )
        return (image_part, text_part)

    held_text = shifted(unit_txt, "outer", -HALF)
    anchor = (my_outer + HALF) % outer_count
    image_sum, carried = tile_terms(held_text, anchor)
    for repeat in range(2 * HALF):
        held_text, carried = (
            shifted(held_text.astype(jnp.float32), "outer", 1).astype(held_text.dtype),
            shifted(carried, "outer", 1),
        )
        anchor = (anchor + outer_count - 1) % outer_count
        image_part, text_part = tile_terms(held_text, anchor)
        image_sum = image_sum + image_part
        carried = carried + text_part
    text_total = shifted(carried, "outer", -HALF)
    image_total = lax.psum_scatter(image_sum, "inner", scatter_dimension=0, tiled=True)
    return (
        project_back(inverse_img, full_img, image_total),
        project_back(inverse_txt, full_txt, text_total),
    )


def solution(mesh):
    return jax.shard_map(
        local,
        mesh=mesh,
        in_specs=(P(("outer", "inner"), None), P(("outer", "inner"), None), P(), P()),
        out_specs=(P(("outer", "inner"), None), P(("outer", "inner"), None)),
        check_vma=False,
    )
```

profile of v0, /device:TPU:40, one launch (start us, length us, event | category | flops | bytes accessed | tf_op | source)
XLA Modules:
  0.0 316.5 jit_solution(14558476606302675334)
XLA Ops:
  9.4 5.0 %collective-permute-start = (bf16[128,1152]{1,0:T(8,128)(2,1)S(1)}, bf16[128,1152]{1,0:T(8,128)(2,1)S(1)}, u32[]{:S(2)}, u32[]{:S(2)}) collective-permute-start(bf16[128,1152]{1,0:T(8,128)(2,1)S(1)} %fusion.72), channel_id=1, source_target_pairs={{0,696},{24,720},{48,744},{72,0},{96,24},{120,48},{144,72},{168,96... | collective-permute-start | bytes 884744 | tf_op jit(solution)/shard_map/ppermute | solution.py:13
  17.6 69.4 %all_gather.3 = bf16[384,1152]{1,0:T(8,128)(2,1)S(1)} all-gather(bf16[16,1152]{1,0:T(8,128)(2,1)S(1)} %fusion.90), channel_id=1, replica_groups=mesh['outer'=32,'inner'=24] {'inner'}, dimensions={0}, use_global_device_ids=true | all-gather | bytes 921600 | tf_op jit(solution)/shard_map/all_gather | solution.py:40
  87.0 1.9 collective-permute-start.1
  89.7 1.9 collective-permute-start.7
  91.7 16.3 %collective-permute-done.1 = bf16[128,1152]{1,0:T(8,128)(2,1)S(1)} collective-permute-done((bf16[128,1152]{1,0:T(8,128)(2,1)S(1)}, bf16[128,1152]{1,0:T(8,128)(2,1)S(1)}, u32[]{:S(2)}, u32[]{:S(2)}) %collective-permute-start.1) | collective-permute-done | bytes 294944 | tf_op jit(solution)/shard_map/ppermute | solution.py:13
  108.0 1.9 collective-permute-start.2
  110.7 6.5 %collective-permute-done.7 = f32[128,1152]{1,0:T(8,128)S(1)} collective-permute-done((f32[128,1152]{1,0:T(8,128)S(1)}, f32[128,1152]{1,0:T(8,128)S(1)}, u32[]{:S(2)}, u32[]{:S(2)}) %collective-permute-start.7) | collective-permute-done | bytes 589856 | tf_op jit(solution)/shard_map/ppermute | solution.py:13
  117.6 1.9 collective-permute-start.8
  123.5 13.8 %collective-permute-done.3 = bf16[128,1152]{1,0:T(8,128)(2,1)S(1)} collective-permute-done((bf16[128,1152]{1,0:T(8,128)(2,1)S(1)}, bf16[128,1152]{1,0:T(8,128)(2,1)S(1)}, u32[]{:S(2)}, u32[]{:S(2)}) %collective-permute-start.3) | collective-permute-done | bytes 294944 | tf_op jit(solution)/shard_map/ppermute | solution.py:13
  137.3 1.9 collective-permute-start.4
  140.2 1.9 collective-permute-start.9
  142.1 7.6 %collective-permute-done.4 = bf16[128,1152]{1,0:T(8,128)(2,1)S(1)} collective-permute-done((bf16[128,1152]{1,0:T(8,128)(2,1)S(1)}, bf16[128,1152]{1,0:T(8,128)(2,1)S(1)}, u32[]{:S(2)}, u32[]{:S(2)}) %collective-permute-start.4) | collective-permute-done | bytes 294944 | tf_op jit(solution)/shard_map/ppermute | solution.py:13
  152.4 12.7 %collective-permute-done.5 = bf16[128,1152]{1,0:T(8,128)(2,1)S(1)} collective-permute-done((bf16[128,1152]{1,0:T(8,128)(2,1)S(1)}, bf16[128,1152]{1,0:T(8,128)(2,1)S(1)}, u32[]{:S(2)}, u32[]{:S(2)}) %collective-permute-start.5) | collective-permute-done | bytes 294944 | tf_op jit(solution)/shard_map/ppermute | solution.py:13
  167.9 10.9 %collective-permute-done.6 = bf16[128,1152]{1,0:T(8,128)(2,1)S(1)} collective-permute-done((bf16[128,1152]{1,0:T(8,128)(2,1)S(1)}, bf16[128,1152]{1,0:T(8,128)(2,1)S(1)}, u32[]{:S(2)}, u32[]{:S(2)}) %collective-permute-start.6) | collective-permute-done | bytes 294944 | tf_op jit(solution)/shard_map/ppermute | solution.py:13
  179.6 2.0 fusion.5
  182.1 1.9 collective-permute-start.10
  184.4 15.0 %collective-permute-done.10 = f32[128,1152]{1,0:T(8,128)S(1)} collective-permute-done((f32[128,1152]{1,0:T(8,128)S(1)}, f32[128,1152]{1,0:T(8,128)S(1)}, u32[]{:S(2)}, u32[]{:S(2)}) %collective-permute-start.10) | collective-permute-done | bytes 589856 | tf_op jit(solution)/shard_map/ppermute | solution.py:13
  199.5 1.9 collective-permute-start.11
  201.8 14.8 %collective-permute-done.11 = f32[128,1152]{1,0:T(8,128)S(1)} collective-permute-done((f32[128,1152]{1,0:T(8,128)S(1)}, f32[128,1152]{1,0:T(8,128)S(1)}, u32[]{:S(2)}, u32[]{:S(2)}) %collective-permute-start.11) | collective-permute-done | bytes 589856 | tf_op jit(solution)/shard_map/ppermute | solution.py:13
  216.6 2.1 collective-permute-start.12
  219.1 17.1 %collective-permute-done.12 = f32[128,1152]{1,0:T(8,128)S(1)} collective-permute-done((f32[128,1152]{1,0:T(8,128)S(1)}, f32[128,1152]{1,0:T(8,128)S(1)}, u32[]{:S(2)}, u32[]{:S(2)}) %collective-permute-start.12) | collective-permute-done | bytes 589856 | tf_op jit(solution)/shard_map/ppermute | solution.py:13
  236.2 1.9 collective-permute-start.13
  238.2 19.5 %collective-permute-done.13 = f32[128,1152]{1,0:T(8,128)S(1)} collective-permute-done((f32[128,1152]{1,0:T(8,128)S(1)}, f32[128,1152]{1,0:T(8,128)S(1)}, u32[]{:S(2)}, u32[]{:S(2)}) %collective-permute-start.13) | collective-permute-done | bytes 589856 | tf_op jit(solution)/shard_map/ppermute | solution.py:13
  258.9 48.0 %reduce-scatter.2.cloned.1.call-done = f32[16,1152]{1,0:T(8,128)} async-done(((f32[384,1152]{1,0:T(8,128)}), f32[16,1152]{1,0:T(8,128)}) %reduce-scatter.2.cloned.1.call-update) | async-done | bytes 73744 | tf_op jit(solution)/shard_map/reduce_scatter | solution.py:75
  (50 shorter events, 22.9 us)
Async XLA Ops:
  7.2 299.8 %reduce-scatter.2.cloned.1.call-start = ((), (), s32[]{:S(2)}) async-start(), calls=%async_computation.1 | async-start | bytes 1843200 | tf_op jit(solution)/shard_map/reduce_scatter | solution.py:75
  9.4 77.6 %collective-permute-start = (bf16[128,1152]{1,0:T(8,128)(2,1)S(1)}, bf16[128,1152]{1,0:T(8,128)(2,1)S(1)}, u32[]{:S(2)}, u32[]{:S(2)}) collective-permute-start(bf16[128,1152]{1,0:T(8,128)(2,1)S(1)} %fusion.72), channel_id=1, source_target_pairs={{0,696},{24,720},{48,744},{72,0},{96,24},{120,48},{144,72},{168,96... | collective-permute-start | bytes 884744 | tf_op jit(solution)/shard_map/ppermute | solution.py:13
  87.0 21.0 %collective-permute-start.1 = (bf16[128,1152]{1,0:T(8,128)(2,1)S(1)}, bf16[128,1152]{1,0:T(8,128)(2,1)S(1)}, u32[]{:S(2)}, u32[]{:S(2)}) collective-permute-start(bf16[128,1152]{1,0:T(8,128)(2,1)S(1)} %collective-permute-done), channel_id=1, source_target_pairs={{0,24},{24,48},{48,72},{72,96},{96,120},{120,144},{144,168},{168,1... | collective-permute-start | bytes 884744 | tf_op jit(solution)/shard_map/ppermute | solution.py:13
  89.7 27.5 %collective-permute-start.7 = (f32[128,1152]{1,0:T(8,128)S(1)}, f32[128,1152]{1,0:T(8,128)S(1)}, u32[]{:S(2)}, u32[]{:S(2)}) collective-permute-start(f32[128,1152]{1,0:T(8,128)S(1)} %convolution_multiply_fusion.6), channel_id=1, source_target_pairs={{0,24},{24,48},{48,72},{72,96},{96,120},{120,144},{144,168},{168,1... | collective-permute-start | bytes 1769480 | tf_op jit(solution)/shard_map/ppermute | solution.py:13
  108.0 12.4 %collective-permute-start.2 = (bf16[128,1152]{1,0:T(8,128)(2,1)S(1)}, bf16[128,1152]{1,0:T(8,128)(2,1)S(1)}, u32[]{:S(2)}, u32[]{:S(2)}) collective-permute-start(bf16[128,1152]{1,0:T(8,128)(2,1)S(1)} %collective-permute-done.1), channel_id=1, source_target_pairs={{0,24},{24,48},{48,72},{72,96},{96,120},{120,144},{144,168},{168,1... | collective-permute-start | bytes 884744 | tf_op jit(solution)/shard_map/ppermute | solution.py:13
  117.6 22.5 %collective-permute-start.8 = (f32[128,1152]{1,0:T(8,128)S(1)}, f32[128,1152]{1,0:T(8,128)S(1)}, u32[]{:S(2)}, u32[]{:S(2)}) collective-permute-start(f32[128,1152]{1,0:T(8,128)S(1)} %fusion.6), channel_id=1, source_target_pairs={{0,24},{24,48},{48,72},{72,96},{96,120},{120,144},{144,168},{168,1... | collective-permute-start | bytes 1769480 | tf_op jit(solution)/shard_map/ppermute | solution.py:13
  120.4 16.9 %collective-permute-start.3 = (bf16[128,1152]{1,0:T(8,128)(2,1)S(1)}, bf16[128,1152]{1,0:T(8,128)(2,1)S(1)}, u32[]{:S(2)}, u32[]{:S(2)}) collective-permute-start(bf16[128,1152]{1,0:T(8,128)(2,1)S(1)} %collective-permute-done.2), channel_id=1, source_target_pairs={{0,24},{24,48},{48,72},{72,96},{96,120},{120,144},{144,168},{168,1... | collective-permute-start | bytes 884744 | tf_op jit(solution)/shard_map/ppermute | solution.py:13
  137.3 12.3 %collective-permute-start.4 = (bf16[128,1152]{1,0:T(8,128)(2,1)S(1)}, bf16[128,1152]{1,0:T(8,128)(2,1)S(1)}, u32[]{:S(2)}, u32[]{:S(2)}) collective-permute-start(bf16[128,1152]{1,0:T(8,128)(2,1)S(1)} %collective-permute-done.3), channel_id=1, source_target_pairs={{0,24},{24,48},{48,72},{72,96},{96,120},{120,144},{144,168},{168,1... | collective-permute-start | bytes 884744 | tf_op jit(solution)/shard_map/ppermute | solution.py:13
  140.2 41.9 %collective-permute-start.9 = (f32[128,1152]{1,0:T(8,128)S(1)}, f32[128,1152]{1,0:T(8,128)S(1)}, u32[]{:S(2)}, u32[]{:S(2)}) collective-permute-start(f32[128,1152]{1,0:T(8,128)S(1)} %add.206), channel_id=1, source_target_pairs={{0,24},{24,48},{48,72},{72,96},{96,120},{120,144},{144,168},{168,1... | collective-permute-start | bytes 1769480 | tf_op jit(solution)/shard_map/ppermute | solution.py:13
  149.7 15.5 %collective-permute-start.5 = (bf16[128,1152]{1,0:T(8,128)(2,1)S(1)}, bf16[128,1152]{1,0:T(8,128)(2,1)S(1)}, u32[]{:S(2)}, u32[]{:S(2)}) collective-permute-start(bf16[128,1152]{1,0:T(8,128)(2,1)S(1)} %collective-permute-done.4), channel_id=1, source_target_pairs={{0,24},{24,48},{48,72},{72,96},{96,120},{120,144},{144,168},{168,1... | collective-permute-start | bytes 884744 | tf_op jit(solution)/shard_map/ppermute | solution.py:13
  165.1 13.7 %collective-permute-start.6 = (bf16[128,1152]{1,0:T(8,128)(2,1)S(1)}, bf16[128,1152]{1,0:T(8,128)(2,1)S(1)}, u32[]{:S(2)}, u32[]{:S(2)}) collective-permute-start(bf16[128,1152]{1,0:T(8,128)(2,1)S(1)} %collective-permute-done.5), channel_id=1, source_target_pairs={{0,24},{24,48},{48,72},{72,96},{96,120},{120,144},{144,168},{168,1... | collective-permute-start | bytes 884744 | tf_op jit(solution)/shard_map/ppermute | solution.py:13
  182.1 17.3 %collective-permute-start.10 = (f32[128,1152]{1,0:T(8,128)S(1)}, f32[128,1152]{1,0:T(8,128)S(1)}, u32[]{:S(2)}, u32[]{:S(2)}) collective-permute-start(f32[128,1152]{1,0:T(8,128)S(1)} %add.207), channel_id=1, source_target_pairs={{0,24},{24,48},{48,72},{72,96},{96,120},{120,144},{144,168},{168,1... | collective-permute-start | bytes 1769480 | tf_op jit(solution)/shard_map/ppermute | solution.py:13
  199.5 17.1 %collective-permute-start.11 = (f32[128,1152]{1,0:T(8,128)S(1)}, f32[128,1152]{1,0:T(8,128)S(1)}, u32[]{:S(2)}, u32[]{:S(2)}) collective-permute-start(f32[128,1152]{1,0:T(8,128)S(1)} %add.208), channel_id=1, source_target_pairs={{0,24},{24,48},{48,72},{72,96},{96,120},{120,144},{144,168},{168,1... | collective-permute-start | bytes 1769480 | tf_op jit(solution)/shard_map/ppermute | solution.py:13
  216.6 41.1 %copy-start = (bf16[128,1152]{1,0:T(8,128)(2,1)S(1)}, bf16[128,1152]{1,0:T(8,128)(2,1)}, u32[]{:S(2)}) copy-start(bf16[128,1152]{1,0:T(8,128)(2,1)} %param.5) | copy-start | bytes 884740
  216.6 19.5 %collective-permute-start.12 = (f32[128,1152]{1,0:T(8,128)S(1)}, f32[128,1152]{1,0:T(8,128)S(1)}, u32[]{:S(2)}, u32[]{:S(2)}) collective-permute-start(f32[128,1152]{1,0:T(8,128)S(1)} %add.209), channel_id=1, source_target_pairs={{0,24},{24,48},{48,72},{72,96},{96,120},{120,144},{144,168},{168,1... | collective-permute-start | bytes 1769480 | tf_op jit(solution)/shard_map/ppermute | solution.py:13
  219.1 87.9 %copy-start.1 = (bf16[16,1152]{1,0:T(8,128)(2,1)S(1)}, bf16[16,1152]{1,0:T(8,128)(2,1)}, u32[]{:S(2)}) copy-start(bf16[16,1152]{1,0:T(8,128)(2,1)} %param.4) | copy-start | bytes 110596
  236.2 21.4 %collective-permute-start.13 = (f32[128,1152]{1,0:T(8,128)S(1)}, f32[128,1152]{1,0:T(8,128)S(1)}, u32[]{:S(2)}, u32[]{:S(2)}) collective-permute-start(f32[128,1152]{1,0:T(8,128)S(1)} %add.210), channel_id=1, source_target_pairs={{0,696},{24,720},{48,744},{72,0},{96,24},{120,48},{144,72},{168,96... | collective-permute-start | bytes 1769480 | tf_op jit(solution)/shard_map/ppermute | solution.py:13
Sparse Core Ops, SparseCore 0:
  181.8 125.1 reduce-scatter.1
where the time goes:
time: 317 us; the launch traced here: 316 us
  waiting for transfers between devices  183 us (58%)
  blocking collectives  69.4 us (22%)
  starting transfers between devices  30.1 us (9%)
  between operations  15.7 us (5%)
  matrix products  10 us (3%)
  other arithmetic  8.2 us (3%)
    ppermute x14, waiting for transfers between devices, shifted(): return lax.ppermute(x, axis, [(i, (i + by) % size) for i in range(size)])  135 us
    all_gather x1, blocking collectives, local(): lax.all_gather(full_img.astype(jnp.bfloat16), 'inner', axis=0, tiled=True)  69.4 us
    reduce_scatter x1, waiting for transfers between devices, local(): lax.psum_scatter(image_sum, 'inner', scatter_dimension=0, tiled=True)  48 us
    ppermute x14, starting transfers between devices, shifted(): return lax.ppermute(x, axis, [(i, (i + by) % size) for i in range(size)])  30.1 us
  transfers between devices with their start and end apart: 15, of which 12 were waited for; matrix products, arithmetic and copies ran while one was open for 4% of the time, Pallas kernels for 0%

commit v1 on v0

v1 whole, which is shorter than its diff:
```python
import functools
import math

import jax
import jax.numpy as jnp
from jax import lax
from jax.experimental import pallas as pl
from jax.experimental.pallas import tpu as pltpu
from jax.sharding import PartitionSpec as P

MESH = pl.DeviceIdType.MESH
HALF = 3
D = 1152
IMG = 16
TXT = 128
NO, NI = 32, 24
NZ = 12

STAGE_Z = ((0, 1, -1, 2, -2), (3, -3, 4, -4), (5, -5, 6))
STAGES = tuple(tuple((dz, dy) for dy in (0, 1) for dz in zs) for zs in STAGE_Z)
SLOTS = tuple(slot for stage in STAGES for slot in stage)
INDEX = {slot: n for n, slot in enumerate(SLOTS)}
STAGE_AT = (0, 10, 18, 24)
FAR_Z = (6, 5, -5, 4, -4)
Z_SLOTS = (1, -1, 2, -2, 3, -3, 4, -4, 5, -5, 6)
Z_INDEX = {dz: n for n, dz in enumerate(Z_SLOTS)}


def sign(value):
    return (value > 0) - (value < 0)


def gather_parent(slot):
    dz, dy = slot
    if dz == 0:
        return (0, 0)
    return (sign(dz) * ((abs(dz) - 1) // 2 * 2), dy)


KIDS = {
    slot: tuple(kid for kid in reversed(SLOTS) if kid != (0, 0) and gather_parent(kid) == slot)
    for slot in SLOTS
}


def unit_rows(values):
    widened = values.astype(jnp.float32)
    inverse = lax.rsqrt(jnp.sum(widened * widened, axis=-1, keepdims=True) + 1e-06)
    return inverse, widened * inverse


def project_back(inverse, unit_full, gradient):
    along = jnp.sum(unit_full * gradient, axis=-1, keepdims=True)
    return inverse * (gradient - unit_full * along)


def kernel(
    scale_ref, bias_ref, img_hbm, txt_hbm, gi_ref, gt_ref,
    img_in, txt_in, img, txt, img_acc, txt_acc,
    y_send, y_recv, z_send, z_recv, g_send, g_recv, p_recv,
    in_sem, ag_ss, ag_rs, t_ss, t_rs, y_ss, y_rs, z_ss, z_rs, g_ss, g_rs, p_ss, p_rs,
):
    o = lax.axis_index("outer")
    i = lax.axis_index("inner")
    core = o % 2
    x = (o // 2) % 4
    z = i // 2
    yl = i % 2
    divisor = 1.0 / math.sqrt((2 * HALF + 1) * NI * TXT)

    def along_z(dz, flip):
        return (o, ((z + dz + NZ) % NZ) * 2 + (1 - yl if flip else yl))

    last = (x // 3) * yl
    first = ((3 - x) // 3) * yl
    partner = (o + 1 - 2 * core, i)
    up = ((o + 2 - 8 * last + NO) % NO, i)
    down = ((o - 2 + 8 * first + NO) % NO, i)
    true_up = ((o + 2) % NO, i)
    true_down = ((o - 2 + NO) % NO, i)
    far = ((o - 1 + 2 * core + NO) % NO, i)
    up_row = ((o + 8) % NO, i)
    down_row = ((o - 8 + NO) % NO, i)

    barrier = pltpu.get_barrier_semaphore()

    def greet(device):
        pl.semaphore_signal(barrier, inc=1, device_id=device, device_id_type=MESH)

    peers = [along_z(0, True)] + [along_z(dz, False) for dz in (1, -1, 2, -2, 3, -3)]
    peers += [partner, far, true_up, true_down]
    for peer in peers:
        greet(peer)

    @pl.when(yl == 1)
    def _():
        @pl.when(x == 0)
        def _():
            greet(((o + 6) % NO, i))
            greet(up_row)
            greet(down_row)

        @pl.when(x == 3)
        def _():
            greet(((o - 6 + NO) % NO, i))
            greet(up_row)
            greet(down_row)

    load_img = pltpu.make_async_copy(img_hbm, img_in, in_sem.at[0])
    load_txt = pltpu.make_async_copy(txt_hbm, txt_in, in_sem.at[1])
    load_img.start()
    load_txt.start()
    load_img.wait()
    _, full = unit_rows(img_in[...])
    img[0:IMG, :] = full.astype(jnp.bfloat16)

    through = yl * (1 - ((x + 1) // 2) % 2)
    pl.semaphore_wait(barrier, len(peers) + 3 * through)

    def gather_copy(kid):
        dz, dy = kid
        pz, py = gather_parent(kid)
        a, b = INDEX[(pz, py)], INDEX[kid]
        return pltpu.make_async_remote_copy(
            src_ref=img.at[a * IMG:(a + 1) * IMG],
            dst_ref=img.at[b * IMG:(b + 1) * IMG],
            send_sem=ag_ss.at[b],
            recv_sem=ag_rs.at[b],
            device_id=along_z(dz - pz, dy != py),
            device_id_type=MESH,
        )

    def pass_on(slot):
        if slot != (0, 0):
            gather_copy(slot).wait_recv()
        for kid in KIDS[slot]:
            gather_copy(kid).start()

    def text_copy(source, slot, n, device):
        return pltpu.make_async_remote_copy(
            src_ref=txt.at[source],
            dst_ref=txt.at[slot],
            send_sem=t_ss.at[n],
            recv_sem=t_rs.at[slot],
            device_id=device,
            device_id_type=MESH,
        )

    text_partner = text_copy(0, 1, 1, partner)
    text_up = text_copy(0, 2 + 5 * last, 2, up)
    text_down = text_copy(0, 3 + 5 * first, 3, down)
    text_four = text_copy(2, 4, 4, partner)
    text_five = text_copy(3, 5, 5, partner)
    text_far = text_copy(3 - core, 6, 6, far)
    text_up_row = text_copy(7, 2, 7, up_row)
    text_down_row = text_copy(8, 3, 8, down_row)

    def text_arrived(slot):
        text_copy(0, slot, 0, partner).wait_recv()

    pass_on((0, 0))
    load_txt.wait()
    _, full = unit_rows(txt_in[...])
    txt[0] = full.astype(jnp.bfloat16)
    text_up.start()
    text_down.start()
    text_partner.start()
    pass_on((0, 1))

    factor = scale_ref[0]
    offset = bias_ref[0]

    def tile(stage, slots, first_rows, first_cols):
        r0, r1 = STAGE_AT[stage] * IMG, STAGE_AT[stage + 1] * IMG
        s0, n = slots[0], len(slots)
        rows = img[r0:r1, :]
        cols = txt[s0:s0 + n].reshape(n * TXT, D)
        logits = lax.dot_general(
            rows, cols, (((1,), (1,)), ((), ())), preferred_element_type=jnp.float32
        ) * factor + offset
        if stage == 0 and s0 == 0:
            shape = (r1 - r0, n * TXT)
            r = lax.broadcasted_iota(jnp.int32, shape, 0)
            c = lax.broadcasted_iota(jnp.int32, shape, 1)
            matched = jnp.logical_and(r == c, r < IMG)
            label = jnp.where(matched, 1.0, -1.0)
            weights = -label / (1.0 + jnp.exp(label * logits)) * divisor
        else:
            weights = divisor / (1.0 + jnp.exp(-logits))
        weights = weights.astype(jnp.bfloat16)
        image_part = jnp.dot(weights, cols, preferred_element_type=jnp.float32)
        text_part = lax.dot_general(
            weights, rows, (((0,), (0,)), ((), ())), preferred_element_type=jnp.float32
        ).reshape(n, TXT, D)
        if first_rows:
            img_acc[r0:r1, :] = image_part
        else:
            img_acc[r0:r1, :] += image_part
        if first_cols:
            txt_acc[s0:s0 + n] = text_part
        else:
            txt_acc[s0:s0 + n] += text_part

    pass_on((2, 0))
    pass_on((-2, 0))

    def relay(here, slot, onward):
        @pl.when(yl == 1)
        def _():
            @pl.when(x == here)
            def _():
                text_arrived(slot)
                onward.start()

    relay(0, 7, text_up_row)
    relay(3, 8, text_down_row)
    pass_on((2, 1))
    pass_on((-2, 1))
    for slot in ((1, 0), (-1, 0), (1, 1), (-1, 1)):
        pass_on(slot)
    text_arrived(1)
    tile(0, (0, 1), True, True)
    for slot in ((4, 0), (-4, 0), (4, 1), (-4, 1)):
        pass_on(slot)
    text_arrived(2)
    text_arrived(3)
    text_far.start()
    text_four.start()
    text_five.start()
    tile(0, (2, 3), False, True)
    for slot in ((3, 0), (-3, 0), (3, 1), (-3, 1)):
        pass_on(slot)
    tile(1, (0, 1), True, False)
    tile(1, (2, 3), False, False)
    text_arrived(4)
    text_arrived(5)
    tile(0, (4, 5), False, True)
    tile(1, (4, 5), False, False)
    text_arrived(6)
    tile(0, (6,), False, True)
    tile(1, (6,), False, False)
    for slot in STAGES[2]:
        pass_on(slot)

    def grad_copy(source, slot, n, device):
        return pltpu.make_async_remote_copy(
            src_ref=source,
            dst_ref=g_recv.at[slot],
            send_sem=g_ss.at[n],
            recv_sem=g_rs.at[slot],
            device_id=device,
            device_id_type=MESH,
        )

    def pair_copy(slot, n):
        return pltpu.make_async_remote_copy(
            src_ref=txt_acc.at[slot],
            dst_ref=p_recv.at[n],
            send_sem=p_ss.at[n],
            recv_sem=p_rs.at[n],
            device_id=partner,
            device_id_type=MESH,
        )

    grad_far = grad_copy(g_send.at[2], 2, 2, far)
    grad_up = grad_copy(g_send.at[1], 3 * last, 0, up)
    grad_down = grad_copy(g_send.at[0], 1 + 3 * first, 1, down)
    grad_up_row = grad_copy(g_recv.at[3], 0, 3, up_row)
    grad_down_row = grad_copy(g_recv.at[4], 1, 4, down_row)
    pair_own, pair_four, pair_five = pair_copy(1, 0), pair_copy(4, 1), pair_copy(5, 2)

    def grad_arrived(slot):
        grad_copy(g_send.at[0], slot, 0, partner).wait_recv()

    def y_copy(stage):
        a, b = STAGE_AT[stage] * IMG // 2, STAGE_AT[stage + 1] * IMG // 2
        return pltpu.make_async_remote_copy(
            src_ref=y_send.at[a:b],
            dst_ref=y_recv.at[a:b],
            send_sem=y_ss.at[stage],
            recv_sem=y_rs.at[stage],
            device_id=along_z(0, True),
            device_id_type=MESH,
        )

    def y_start(stage):
        a, b = STAGE_AT[stage] * IMG // 2, STAGE_AT[stage + 1] * IMG // 2
        y_send[a:b, :] = img_acc[a + b:2 * b, :].astype(jnp.bfloat16)
        y_copy(stage).start()

    def z_copy(dz):
        n = Z_INDEX[dz]
        hop = dz - sign(dz) * 3 if abs(dz) > 3 else dz
        return pltpu.make_async_remote_copy(
            src_ref=z_send.at[n],
            dst_ref=z_recv.at[n],
            send_sem=z_ss.at[n],
            recv_sem=z_rs.at[n],
            device_id=along_z(-hop, False),
            device_id_type=MESH,
        )

    def y_sum(dz):
        stage = 0 if abs(dz) < 3 else 1 if abs(dz) < 5 else 2
        a = INDEX[(dz, 0)] * IMG
        b = STAGE_AT[stage] * IMG // 2 + STAGE_Z[stage].index(dz) * IMG
        return img_acc[a:a + IMG, :] + y_recv[b:b + IMG, :].astype(jnp.float32)

    def z_start(dz, total):
        z_send[Z_INDEX[dz]] = total.astype(jnp.bfloat16)
        z_copy(dz).start()

    def z_got(dz):
        z_copy(dz).wait_recv()
        return z_recv[Z_INDEX[dz]].astype(jnp.float32)

    tile(2, (6,), True, False)
    g_send[2] = txt_acc[6].astype(jnp.bfloat16)
    grad_far.start()
    tile(2, (4, 5), False, False)
    pair_four.start()
    pair_five.start()
    tile(2, (2, 3), False, False)
    tile(2, (0, 1), False, False)
    y_start(2)
    y_start(1)
    y_start(0)
    pair_own.start()

    pair_four.wait_recv()
    g_send[0] = (txt_acc[2] + p_recv[1]).astype(jnp.bfloat16)
    pair_five.wait_recv()
    g_send[1] = (txt_acc[3] + p_recv[2]).astype(jnp.bfloat16)
    grad_arrived(2)

    @pl.when(core == 1)
    def _():
        g_send[0] = (txt_acc[2] + p_recv[1] + g_recv[2].astype(jnp.float32)).astype(jnp.bfloat16)

    @pl.when(core == 0)
    def _():
        g_send[1] = (txt_acc[3] + p_recv[2] + g_recv[2].astype(jnp.float32)).astype(jnp.bfloat16)

    grad_down.start()
    grad_up.start()

    y_copy(2).wait_recv()
    for dz in (6, 5, -5):
        z_start(dz, y_sum(dz))
    y_copy(1).wait_recv()
    for dz in (4, -4):
        z_start(dz, y_sum(dz))
    y_copy(0).wait_recv()
    for dz in (2, -2, 1, -1):
        z_start(dz, y_sum(dz))

    @pl.when(yl == 1)
    def _():
        @pl.when(x == 0)
        def _():
            grad_arrived(3)
            grad_up_row.start()

        @pl.when(x == 3)
        def _():
            grad_arrived(4)
            grad_down_row.start()

    z_start(3, y_sum(3) + z_got(4) + z_got(5) + z_got(6))
    z_start(-3, y_sum(-3) + z_got(-4) + z_got(-5))

    pair_own.wait_recv()
    text_total = txt_acc[0] + p_recv[0]
    grad_arrived(0)
    grad_arrived(1)
    text_total = text_total + (g_recv[0].astype(jnp.float32) + g_recv[1].astype(jnp.float32))
    inverse, full = unit_rows(txt_in[...])
    gt_ref[...] = project_back(inverse, full, text_total * factor)

    image_total = y_sum(0)
    for dz in (1, -1, 2, -2, 3, -3):
        image_total = image_total + z_got(dz)
    inverse, full = unit_rows(img_in[...])
    gi_ref[...] = project_back(inverse, full, image_total * factor)

    for slot in SLOTS[1:]:
        gather_copy(slot).wait_send()
    for copy in (
        text_partner, text_up, text_down, text_four, text_five, text_far,
        grad_far, grad_up, grad_down, pair_own, pair_four, pair_five,
        y_copy(0), y_copy(1), y_copy(2),
    ):
        copy.wait_send()
    for dz in Z_SLOTS:
        z_copy(dz).wait_send()

    @pl.when(yl == 1)
    def _():
        @pl.when(x == 0)
        def _():
            text_up_row.wait_send()
            grad_up_row.wait_send()

        @pl.when(x == 3)
        def _():
            text_down_row.wait_send()
            grad_down_row.wait_send()


def local(images, texts, logit_scale, logit_bias):
    bf, f32 = jnp.bfloat16, jnp.float32
    dma = pltpu.SemaphoreType.DMA
    return pl.pallas_call(
        kernel,
        out_shape=(
            jax.ShapeDtypeStruct((IMG, D), f32),
            jax.ShapeDtypeStruct((TXT, D), f32),
        ),
        in_specs=[pl.BlockSpec(memory_space=pltpu.SMEM)] * 2
        + [pl.BlockSpec(memory_space=pl.ANY)] * 2,
        out_specs=[pl.BlockSpec(memory_space=pltpu.VMEM)] * 2,
        scratch_shapes=[
            pltpu.VMEM((IMG, D), bf),
            pltpu.VMEM((TXT, D), bf),
            pltpu.VMEM((NI * IMG, D), bf),
            pltpu.VMEM((9, TXT, D), bf),
            pltpu.VMEM((NI * IMG, D), f32),
            pltpu.VMEM((7, TXT, D), f32),
            pltpu.VMEM((NI * IMG // 2, D), bf),
            pltpu.VMEM((NI * IMG // 2, D), bf),
            pltpu.VMEM((11, IMG, D), bf),
            pltpu.VMEM((11, IMG, D), bf),
            pltpu.VMEM((3, TXT, D), bf),
            pltpu.VMEM((5, TXT, D), bf),
            pltpu.VMEM((3, TXT, D), f32),
            dma((2,)),
            dma((NI,)), dma((NI,)),
            dma((9,)), dma((9,)),
            dma((3,)), dma((3,)),
            dma((11,)), dma((11,)),
            dma((5,)), dma((5,)),
            dma((3,)), dma((3,)),
        ],
        compiler_params=pltpu.CompilerParams(
            collective_id=0, has_side_effects=True, vmem_limit_bytes=48 << 20
        ),
        name="pair_gradients",
    )(logit_scale, logit_bias, images, texts)


def solution(mesh):
    return jax.shard_map(
        local,
        mesh=mesh,
        in_specs=(P(("outer", "inner"), None), P(("outer", "inner"), None), P(), P()),
        out_specs=(P(("outer", "inner"), None), P(("outer", "inner"), None)),
        check_vma=False,
    )
```

time: 317 us -> 79.4 us (0.25)
  waiting for transfers between devices: 183 us -> 0 us
  Pallas kernels: 0 us -> 74 us
  blocking collectives: 69.4 us -> 0 us
  starting transfers between devices: 30.1 us -> 0 us
  between operations: 15.7 us -> 1.94 us
  matrix products: 10 us -> 0 us
  other arithmetic: 8.2 us -> 0 us
    ppermute x14 -> x0, waiting for transfers between devices: 135 us -> none  [shifted(): return lax.ppermute(x, axis, [(i, (i + by) % size) for i in range(size)])]
    pallas_call x0 -> x1, Pallas kernels: none -> 74 us  [local(): pl.pallas_call(kernel, out_shape=(jax.ShapeDtypeStruct((IMG, D), f32), ja...]
    all_gather x1 -> x0, blocking collectives: 69.4 us -> none  [local(): lax.all_gather(full_img.astype(jnp.bfloat16), 'inner', axis=0, tiled=True)]
    reduce_scatter x1 -> x0, waiting for transfers between devices: 48 us -> none  [local(): lax.psum_scatter(image_sum, 'inner', scatter_dimension=0, tiled=True)]
    ppermute x14 -> x0, starting transfers between devices: 30.1 us -> none  [shifted(): return lax.ppermute(x, axis, [(i, (i + by) % size) for i in range(size)])]
    dot_general x21 -> x0, matrix products: 10 us -> none  [the longest x7 4.26 us: tile_terms(): jnp.dot(weights, held_text, preferred_element_type=jnp.float32) * factor]
    reduce_sum x4 -> x0, other arithmetic: 3.29 us -> none  [the longest x2 1.99 us: unit_rows(): jnp.sum(widened * widened, axis=-1, keepdims=True) + 1e-06]
  transfers between devices with their start and end apart: 15 -> 0, of which waited for: 12 -> 0; matrix products, arithmetic and copies ran while one was open for 4% -> 0% of each run, Pallas kernels for 0% -> 0%
where the time goes in v1:
time: 79.4 us; the launch traced here: 79.1 us
  Pallas kernels  74 us (93%)
  local copies, waits for them, and re-layouts  3.17 us (4%)
  between operations  1.94 us (2%)
    pallas_call x1, Pallas kernels, local(): pl.pallas_call(kernel, out_shape=(jax.ShapeDtypeStruct((IMG, D), f32), ja...  74 us
    unnamed x6, local copies, waits for them, and re-layouts  3.17 us

profile of v1, /device:TPU:40, one launch (start us, length us, event | category | flops | bytes accessed | tf_op | source)
XLA Modules:
  0.0 79.1 jit_solution(3707343543985436412)
XLA Ops:
  1.9 0.0 copy-start
  1.9 1.0 %copy-done = bf16[128,1152]{1,0:T(8,128)(2,1)S(1)} copy-done((bf16[128,1152]{1,0:T(8,128)(2,1)S(1)}, bf16[128,1152]{1,0:T(8,128)(2,1)}, u32[]{:S(2)}) %copy-start) | copy-done | bytes 294936
  2.9 0.0 copy-start.1
  2.9 0.8 copy-done.1
  3.7 74.0 %pair_gradients.1 = (f32[16,1152]{1,0:T(8,128)S(1)}, f32[128,1152]{1,0:T(8,128)S(1)}) custom-call(f32[1]{0:T(128)S(6)} %copy.8.scale_ref, f32[1]{0:T(128)S(6)} %copy.9.bias_ref, bf16[16,1152]{1,0:T(8,128)(2,1)S(1)} %copy-done.1, bf16[128,1152]{1,0:T(8,128)(2,1)S(1)} %copy-done), custom_call_target="tpu_custom_call" | custom-call | tf_op jit(solution)/shard_map/pair_gradients/pallas_call | solution.py:413
  77.7 0.6 copy.10
  78.3 0.8 %copy.11 = f32[128,1152]{1,0:T(8,128)} copy(f32[128,1152]{1,0:T(8,128)S(1)} %get-tuple-element.5) | data formatting | bytes 1179648
Async XLA Ops:
  1.9 1.0 %copy-start = (bf16[128,1152]{1,0:T(8,128)(2,1)S(1)}, bf16[128,1152]{1,0:T(8,128)(2,1)}, u32[]{:S(2)}) copy-start(bf16[128,1152]{1,0:T(8,128)(2,1)} %txt_hbm.1) | copy-start | bytes 884740
  2.9 0.8 copy-start.1

commit v2 on v1

v2 whole, which is shorter than its diff:
```python
import functools
import math

import jax
import jax.numpy as jnp
from jax import lax
from jax.experimental import pallas as pl
from jax.experimental.pallas import tpu as pltpu
from jax.sharding import PartitionSpec as P

MESH = pl.DeviceIdType.MESH
HALF = 3
D = 1152
IMG = 16
TXT = 128
NO, NI = 32, 24
NZ = 12

STAGE_Z = ((0, 1, -1, 2, -2), (3, -3, 4, -4), (5, -5, 6))
STAGES = tuple(tuple((dz, dy) for dy in (0, 1) for dz in zs) for zs in STAGE_Z)
SLOTS = tuple(slot for stage in STAGES for slot in stage)
INDEX = {slot: n for n, slot in enumerate(SLOTS)}
STAGE_AT = (0, 10, 18, 24)
PARTS = 4
PART = TXT // PARTS
Z_SLOTS = (1, -1, 2, -2, 3, -3, 4, -4, 5, -5, 6)
Z_INDEX = {dz: n for n, dz in enumerate(Z_SLOTS)}


def sign(value):
    return (value > 0) - (value < 0)


def gather_parent(slot):
    dz, dy = slot
    if dz == 0:
        return (0, 0)
    return (sign(dz) * ((abs(dz) - 1) // 2 * 2), dy)


KIDS = {
    slot: tuple(kid for kid in reversed(SLOTS) if kid != (0, 0) and gather_parent(kid) == slot)
    for slot in SLOTS
}


def unit_rows(values):
    widened = values.astype(jnp.float32)
    inverse = lax.rsqrt(jnp.sum(widened * widened, axis=-1, keepdims=True) + 1e-06)
    return inverse, widened * inverse


def project_back(inverse, unit_full, gradient):
    along = jnp.sum(unit_full * gradient, axis=-1, keepdims=True)
    return inverse * (gradient - unit_full * along)


def kernel(
    scale_hbm, bias_hbm, img_hbm, txt_hbm, gi_ref, gt_ref,
    scale, bias, img_in, txt_in, img, txt, img_acc, txt_acc,
    y_send, y_recv, z_send, z_recv, g_send, g_recv, p_recv,
    in_sem, ag_ss, ag_rs, t_ss, t_rs, y_ss, y_rs, z_ss, z_rs, g_ss, g_rs, p_ss, p_rs,
):
    o = lax.axis_index("outer")
    i = lax.axis_index("inner")
    core = o % 2
    x = (o // 2) % 4
    z = i // 2
    yl = i % 2
    divisor = 1.0 / math.sqrt((2 * HALF + 1) * NI * TXT)

    def along_z(dz, flip):
        return (o, ((z + dz + NZ) % NZ) * 2 + (1 - yl if flip else yl))

    def at(shift):
        return ((o + shift + NO) % NO, i)

    last_x = x // 3
    first_x = (3 - x) // 3
    last = last_x * yl
    first = first_x * yl
    through = last + first
    inner_end = last_x * core + first_x * (1 - core)
    outer_end = (x // 2) * (1 - x % 2) * core + (x % 2) * (1 - x // 2) * (1 - core)
    side = 2 * core - 1

    barrier = pltpu.get_barrier_semaphore()

    def greet(device):
        pl.semaphore_signal(barrier, inc=1, device_id=device, device_id_type=MESH)

    peers = [along_z(0, True)] + [along_z(dz, False) for dz in (1, -1, 2, -2, 3, -3)]
    peers += [at(1 - 2 * core), at(side), at(2), at(-2)]
    for peer in peers:
        greet(peer)

    @pl.when(through == 1)
    def _():
        greet(at(6 * first_x - 6 * last_x))
        greet(at(8))
        greet(at(-8))

    @pl.when(inner_end == 1)
    def _():
        greet(at(3 * side))
        greet(at(-5 * side))

    @pl.when(outer_end == 1)
    def _():
        greet(at(3 * side))
        greet(at(-5 * side))
        greet(at(8))
        greet(at(-8))

    loads = [
        pltpu.make_async_copy(source, target, in_sem.at[n])
        for n, (source, target) in enumerate(
            ((img_hbm, img_in), (txt_hbm, txt_in), (scale_hbm, scale), (bias_hbm, bias))
        )
    ]
    for load in loads:
        load.start()
    loads[0].wait()
    _, full = unit_rows(img_in[...])
    img[0:IMG, :] = full.astype(jnp.bfloat16)

    pl.semaphore_wait(barrier, len(peers) + 3 * through + 2 * inner_end + 4 * outer_end)

    def gather_copy(kid):
        dz, dy = kid
        pz, py = gather_parent(kid)
        a, b = INDEX[(pz, py)], INDEX[kid]
        return pltpu.make_async_remote_copy(
            src_ref=img.at[a * IMG:(a + 1) * IMG],
            dst_ref=img.at[b * IMG:(b + 1) * IMG],
            send_sem=ag_ss.at[b],
            recv_sem=ag_rs.at[b],
            device_id=along_z(dz - pz, dy != py),
            device_id_type=MESH,
        )

    def pass_on(slot):
        if slot != (0, 0):
            gather_copy(slot).wait_recv()
        for kid in KIDS[slot]:
            gather_copy(kid).start()

    def text_copy(source, slot, n, device, part):
        rows = pl.ds(part * PART, PART)
        return pltpu.make_async_remote_copy(
            src_ref=txt.at[source, rows],
            dst_ref=txt.at[slot, rows],
            send_sem=t_ss.at[n, part],
            recv_sem=t_rs.at[slot, part],
            device_id=device,
            device_id_type=MESH,
        )

    def text_copies(source, slot, n, device):
        return [text_copy(source, slot, n, device, part) for part in range(PARTS)]

    partner = at(1 - 2 * core)
    up = at(2 - 8 * last)
    down = at(8 * first - 2)
    text_partner = text_copies(0, 1, 1, partner)
    text_up = text_copies(0, 2 + 5 * last, 2, up)
    text_down = text_copies(0, 3 + 5 * first, 3, down)
    text_four = text_copies(2, 4, 4, partner)
    text_five = text_copies(3, 5, 5, partner)
    text_far = text_copies(3 - core, 6, 6, at(side))
    text_far_own = text_copies(0, 6, 0, at(3 * side))
    text_through = text_copies(7 + last, 2 + last, 7, at(8 * first - 8 * last))

    def text_arrived(slot, part):
        text_copy(0, slot, 0, partner, part).wait_recv()

    def all_arrived(slot):
        for part in range(PARTS):
            text_arrived(slot, part)

    pass_on((0, 0))
    loads[1].wait()
    _, full = unit_rows(txt_in[...])
    txt[0] = full.astype(jnp.bfloat16)
    for part in range(PARTS):
        text_up[part].start()
        text_down[part].start()

    @pl.when(outer_end == 1)
    def _():
        for part in range(PARTS):
            text_far_own[part].start()

    for part in range(PARTS):
        text_partner[part].start()
    pass_on((0, 1))
    loads[2].wait()
    loads[3].wait()
    factor = scale[0]
    offset = bias[0]

    def tile(first_stage, last_stage, slots, first_rows, first_cols):
        r0, r1 = STAGE_AT[first_stage] * IMG, STAGE_AT[last_stage + 1] * IMG
        s0, n = slots[0], len(slots)
        rows = img[r0:r1, :]
        cols = txt[s0:s0 + n].reshape(n * TXT, D)
        logits = lax.dot_general(
            cols, rows, (((1,), (1,)), ((), ())), preferred_element_type=jnp.float32
        ) * factor + offset
        if r0 == 0 and s0 == 0:
            shape = (n * TXT, r1 - r0)
            t = lax.broadcasted_iota(jnp.int32, shape, 0)
            r = lax.broadcasted_iota(jnp.int32, shape, 1)
            matched = jnp.logical_and(r == t, r < IMG)
            label = jnp.where(matched, 1.0, -1.0)
            weights = -label / (1.0 + jnp.exp(label * logits)) * divisor
        else:
            weights = divisor / (1.0 + jnp.exp(-logits))
        weights = weights.astype(jnp.bfloat16)
        text_part = jnp.dot(weights, rows, preferred_element_type=jnp.float32).reshape(n, TXT, D)
        image_part = lax.dot_general(
            weights, cols, (((0,), (0,)), ((), ())), preferred_element_type=jnp.float32
        )
        if first_rows:
            img_acc[r0:r1, :] = image_part
        else:
            img_acc[r0:r1, :] += image_part
        if first_cols:
            txt_acc[s0:s0 + n] = text_part
        else:
            txt_acc[s0:s0 + n] += text_part

    def y_copy(stage):
        a, b = STAGE_AT[stage] * IMG // 2, STAGE_AT[stage + 1] * IMG // 2
        return pltpu.make_async_remote_copy(
            src_ref=y_send.at[a:b],
            dst_ref=y_recv.at[a:b],
            send_sem=y_ss.at[stage],
            recv_sem=y_rs.at[stage],
            device_id=along_z(0, True),
            device_id_type=MESH,
        )

    def y_start(stage):
        a, b = STAGE_AT[stage] * IMG // 2, STAGE_AT[stage + 1] * IMG // 2
        y_send[a:b, :] = img_acc[a + b:2 * b, :].astype(jnp.bfloat16)
        y_copy(stage).start()

    for slot in ((2, 0), (-2, 0), (2, 1), (-2, 1)):
        pass_on(slot)
    for slot in ((1, 0), (-1, 0), (1, 1), (-1, 1)):
        pass_on(slot)
    all_arrived(1)
    tile(0, 0, (0, 1), True, True)

    @pl.when(through == 1)
    def _():
        for part in range(PARTS):
            text_arrived(7 + last, part)
            text_through[part].start()

    for slot in ((4, 0), (-4, 0), (4, 1), (-4, 1)):
        pass_on(slot)
    for part in range(PARTS):
        text_arrived(2, part)
        text_arrived(3, part)

        @pl.when(inner_end == 0)
        def _():
            text_far[part].start()

        text_four[part].start()
        text_five[part].start()
    tile(0, 0, (2, 3), False, True)
    for slot in ((3, 0), (-3, 0), (3, 1), (-3, 1)):
        pass_on(slot)
    tile(1, 1, (0, 1, 2, 3), True, False)
    all_arrived(4)
    all_arrived(5)
    tile(0, 1, (4, 5), False, True)
    all_arrived(6)
    tile(0, 1, (6,), False, True)
    y_start(1)
    y_start(0)
    for slot in STAGES[2]:
        pass_on(slot)

    def grad_copy(source, slot, n, device, part):
        return pltpu.make_async_remote_copy(
            src_ref=source.at[pl.ds(part * PART, PART)],
            dst_ref=g_recv.at[slot, pl.ds(part * PART, PART)],
            send_sem=g_ss.at[n, part],
            recv_sem=g_rs.at[slot, part],
            device_id=device,
            device_id_type=MESH,
        )

    def grad_copies(source, slot, n, device):
        return [grad_copy(source, slot, n, device, part) for part in range(PARTS)]

    def pair_copy(slot, n):
        return pltpu.make_async_remote_copy(
            src_ref=txt_acc.at[slot],
            dst_ref=p_recv.at[n],
            send_sem=p_ss.at[n],
            recv_sem=p_rs.at[n],
            device_id=partner,
            device_id_type=MESH,
        )

    far_shift = side * (1 - inner_end) - 5 * side * inner_end
    early_shift = core * (2 - 8 * last) + (1 - core) * (8 * first - 2)
    late_shift = (1 - core) * (2 - 8 * last) + core * (8 * first - 2)
    early_slot = core * 3 * last + (1 - core) * (1 + 3 * first)
    late_slot = (1 - core) * 3 * last + core * (1 + 3 * first)
    grad_far = grad_copies(g_send.at[2], 2 + 4 * inner_end, 2, at(far_shift))
    grad_early = grad_copies(g_send.at[0], early_slot, 0, at(early_shift))
    grad_late = grad_copies(g_send.at[1], late_slot, 1, at(late_shift))
    grad_through = grad_copies(g_recv.at[3 + last], last, 3, at(8 * first - 8 * last))
    grad_far_through = grad_copies(g_recv.at[6], 5, 4, at(-8 * side))
    pair_own, pair_early, pair_late = pair_copy(1, 0), pair_copy(5 - core, 2 - core), pair_copy(4 + core, 1 + core)

    def grad_arrived(slot, part):
        grad_copy(g_send.at[0], slot, 0, partner, part).wait_recv()

    def pair_arrived(n):
        pair_copy(1, n).wait_recv()

    def z_copy(dz):
        n = Z_INDEX[dz]
        hop = dz - sign(dz) * 3 if abs(dz) > 3 else dz
        return pltpu.make_async_remote_copy(
            src_ref=z_send.at[n],
            dst_ref=z_recv.at[n],
            send_sem=z_ss.at[n],
            recv_sem=z_rs.at[n],
            device_id=along_z(-hop, False),
            device_id_type=MESH,
        )

    def y_sum(dz):
        stage = 0 if abs(dz) < 3 else 1 if abs(dz) < 5 else 2
        a = INDEX[(dz, 0)] * IMG
        b = STAGE_AT[stage] * IMG // 2 + STAGE_Z[stage].index(dz) * IMG
        return img_acc[a:a + IMG, :] + y_recv[b:b + IMG, :].astype(jnp.float32)

    def z_start(dz, total):
        z_send[Z_INDEX[dz]] = total.astype(jnp.bfloat16)
        z_copy(dz).start()

    def z_got(dz):
        z_copy(dz).wait_recv()
        return z_recv[Z_INDEX[dz]].astype(jnp.float32)

    tile(2, 2, (4, 5, 6), True, False)
    pair_early.start()
    g_send[2] = txt_acc[6].astype(jnp.bfloat16)
    for copy in grad_far:
        copy.start()
    pair_late.start()
    tile(2, 2, (0, 1, 2, 3), False, False)
    y_start(2)
    pair_arrived(1 + core)
    for part in range(PARTS):
        rows = pl.ds(part * PART, PART)
        g_send[0, rows] = (txt_acc[2 + core, rows] + p_recv[1 + core, rows]).astype(jnp.bfloat16)
        grad_early[part].start()
    pair_own.start()

    y_copy(1).wait_recv()
    for dz in (4, -4):
        z_start(dz, y_sum(dz))
    y_copy(0).wait_recv()
    for dz in (2, -2, 1, -1):
        z_start(dz, y_sum(dz))
    y_copy(2).wait_recv()
    for dz in (6, 5, -5):
        z_start(dz, y_sum(dz))

    pair_arrived(2 - core)
    for part in range(PARTS):
        rows = pl.ds(part * PART, PART)

        @pl.when(inner_end == 0)
        def _():
            grad_arrived(2, part)
            g_send[1, rows] = (
                txt_acc[3 - core, rows] + p_recv[2 - core, rows] + g_recv[2, rows].astype(jnp.float32)
            ).astype(jnp.bfloat16)

        @pl.when(inner_end == 1)
        def _():
            g_send[1, rows] = (txt_acc[3 - core, rows] + p_recv[2 - core, rows]).astype(jnp.bfloat16)

        grad_late[part].start()

    @pl.when(outer_end == 1)
    def _():
        for part in range(PARTS):
            grad_arrived(6, part)
            grad_far_through[part].start()

    def go_through():
        for part in range(PARTS):
            grad_arrived(3 + last, part)
            grad_through[part].start()

    early_through = first * core + last * (1 - core)
    late_through = first * (1 - core) + last * core

    @pl.when(early_through == 1)
    def _():
        go_through()

    z_start(3, y_sum(3) + z_got(4) + z_got(5) + z_got(6))
    z_start(-3, y_sum(-3) + z_got(-4) + z_got(-5))

    @pl.when(late_through == 1)
    def _():
        go_through()

    inverse, full = unit_rows(img_in[...])
    image_total = y_sum(0)
    for dz in (1, -1, 2, -2, 3, -3):
        image_total = image_total + z_got(dz)
    gi_ref[...] = project_back(inverse, full, image_total * factor)

    pair_arrived(0)
    for part in range(PARTS):
        rows = pl.ds(part * PART, PART)
        grad_arrived(0, part)
        grad_arrived(1, part)
        txt_acc[0, rows] += p_recv[0, rows] + (
            g_recv[0, rows].astype(jnp.float32) + g_recv[1, rows].astype(jnp.float32)
        )

        @pl.when(outer_end == 1)
        def _():
            grad_arrived(5, part)
            txt_acc[0, rows] += g_recv[5, rows].astype(jnp.float32)

        inverse, full = unit_rows(txt_in[rows, :])
        gt_ref[rows, :] = project_back(inverse, full, txt_acc[0, rows] * factor)

    for slot in SLOTS[1:]:
        gather_copy(slot).wait_send()
    for dz in Z_SLOTS:
        z_copy(dz).wait_send()
    for copy in (y_copy(0), y_copy(1), y_copy(2), pair_own, pair_early, pair_late):
        copy.wait_send()
    for copies in (text_partner, text_up, text_down, text_four, text_five, grad_far, grad_early, grad_late):
        for copy in copies:
            copy.wait_send()

    @pl.when(inner_end == 0)
    def _():
        for copy in text_far:
            copy.wait_send()

    @pl.when(outer_end == 1)
    def _():
        for copy in text_far_own + grad_far_through:
            copy.wait_send()

    @pl.when(through == 1)
    def _():
        for copy in text_through + grad_through:
            copy.wait_send()


def local(images, texts, logit_scale, logit_bias):
    bf, f32 = jnp.bfloat16, jnp.float32
    dma = pltpu.SemaphoreType.DMA
    return pl.pallas_call(
        kernel,
        out_shape=(
            jax.ShapeDtypeStruct((IMG, D), f32),
            jax.ShapeDtypeStruct((TXT, D), f32),
        ),
        in_specs=[pl.BlockSpec(memory_space=pl.ANY)] * 4,
        out_specs=[pl.BlockSpec(memory_space=pltpu.VMEM)] * 2,
        scratch_shapes=[
            pltpu.SMEM((1,), f32),
            pltpu.SMEM((1,), f32),
            pltpu.VMEM((IMG, D), bf),
            pltpu.VMEM((TXT, D), bf),
            pltpu.VMEM((NI * IMG, D), bf),
            pltpu.VMEM((9, TXT, D), bf),
            pltpu.VMEM((NI * IMG, D), f32),
            pltpu.VMEM((7, TXT, D), f32),
            pltpu.VMEM((NI * IMG // 2, D), bf),
            pltpu.VMEM((NI * IMG // 2, D), bf),
            pltpu.VMEM((11, IMG, D), bf),
            pltpu.VMEM((11, IMG, D), bf),
            pltpu.VMEM((3, TXT, D), bf),
            pltpu.VMEM((7, TXT, D), bf),
            pltpu.VMEM((3, TXT, D), f32),
            dma((4,)),
            dma((NI,)), dma((NI,)),
            dma((8, PARTS)), dma((9, PARTS)),
            dma((3,)), dma((3,)),
            dma((11,)), dma((11,)),
            dma((5, PARTS)), dma((7, PARTS)),
            dma((3,)), dma((3,)),
        ],
        compiler_params=pltpu.CompilerParams(
            collective_id=0, has_side_effects=True, vmem_limit_bytes=48 << 20
        ),
        name="pair_gradients",
    )(logit_scale, logit_bias, images, texts)


def solution(mesh):
    return jax.shard_map(
        local,
        mesh=mesh,
        in_specs=(P(("outer", "inner"), None), P(("outer", "inner"), None), P(), P()),
        out_specs=(P(("outer", "inner"), None), P(("outer", "inner"), None)),
        check_vma=False,
    )
```

time: 79.4 us -> 71.9 us (0.906)
  the two profiles are of different devices: /device:TPU:40 before, /device:TPU:64 now
where the time goes in v2:
time: 71.9 us; the launch traced here: 71.6 us
  Pallas kernels  66.5 us (92%)
  local copies, waits for them, and re-layouts  3.17 us (4%)
  between operations  1.94 us (3%)
    pallas_call x1, Pallas kernels, local(): pl.pallas_call(kernel, out_shape=(jax.ShapeDtypeStruct((IMG, D), f32), ja...  66.5 us
    unnamed x6, local copies, waits for them, and re-layouts  3.17 us

profile of v2, /device:TPU:64, one launch (start us, length us, event | category | flops | bytes accessed | tf_op | source)
XLA Modules:
  0.0 71.6 jit_solution(14171113317539937859)
XLA Ops:
  1.9 0.0 copy-start
  1.9 1.0 %copy-done = bf16[128,1152]{1,0:T(8,128)(2,1)S(1)} copy-done((bf16[128,1152]{1,0:T(8,128)(2,1)S(1)}, bf16[128,1152]{1,0:T(8,128)(2,1)}, u32[]{:S(2)}) %copy-start) | copy-done | bytes 294936
  2.9 0.0 copy-start.1
  2.9 0.8 %copy-done.1 = bf16[16,1152]{1,0:T(8,128)(2,1)S(1)} copy-done((bf16[16,1152]{1,0:T(8,128)(2,1)S(1)}, bf16[16,1152]{1,0:T(8,128)(2,1)}, u32[]{:S(2)}) %copy-start.1) | copy-done | bytes 36888
  3.7 66.5 %pair_gradients.1 = (f32[16,1152]{1,0:T(8,128)S(1)}, f32[128,1152]{1,0:T(8,128)S(1)}) custom-call(f32[1]{0:T(128)S(6)} %copy.8.scale_hbm, f32[1]{0:T(128)S(6)} %copy.9.bias_hbm, bf16[16,1152]{1,0:T(8,128)(2,1)S(1)} %copy-done.1, bf16[128,1152]{1,0:T(8,128)(2,1)S(1)} %copy-done), custom_call_target="tpu_custom_call" | custom-call | tf_op jit(solution)/shard_map/pair_gradients/pallas_call | solution.py:474
  70.2 0.6 copy.10
  70.8 0.8 %copy.11 = f32[128,1152]{1,0:T(8,128)} copy(f32[128,1152]{1,0:T(8,128)S(1)} %get-tuple-element.5) | data formatting | bytes 1179648
Async XLA Ops:
  1.9 1.0 %copy-start = (bf16[128,1152]{1,0:T(8,128)(2,1)S(1)}, bf16[128,1152]{1,0:T(8,128)(2,1)}, u32[]{:S(2)}) copy-start(bf16[128,1152]{1,0:T(8,128)(2,1)} %txt_hbm.1) | copy-start | bytes 884740
  2.9 0.8 %copy-start.1 = (bf16[16,1152]{1,0:T(8,128)(2,1)S(1)}, bf16[16,1152]{1,0:T(8,128)(2,1)}, u32[]{:S(2)}) copy-start(bf16[16,1152]{1,0:T(8,128)(2,1)} %img_hbm.1) | copy-start | bytes 110596

commit v3 on v2

--- a/solution.py
+++ b/solution.py
@@ -23,23 +23,30 @@
 STAGE_AT = (0, 10, 18, 24)
 PARTS = 4
 PART = TXT // PARTS
-Z_SLOTS = (1, -1, 2, -2, 3, -3, 4, -4, 5, -5, 6)
-Z_INDEX = {dz: n for n, dz in enumerate(Z_SLOTS)}
 
 
 def sign(value):
     return (value > 0) - (value < 0)
 
 
-def gather_parent(slot):
+def tree_parent(slot):
     dz, dy = slot
+    if dz == 6:
+        return (4, 0) if dy == 0 else (-4, 1)
     if dz == 0:
         return (0, 0)
-    return (sign(dz) * ((abs(dz) - 1) // 2 * 2), dy)
+    if dz % 2 == 0:
+        return (dz - 2 * sign(dz), dy)
+    return (dz, 0) if dy else (dz - sign(dz), 0)
 
 
 KIDS = {
-    slot: tuple(kid for kid in reversed(SLOTS) if kid != (0, 0) and gather_parent(kid) == slot)
+    slot: tuple(
+        sorted(
+            (kid for kid in SLOTS if kid != (0, 0) and tree_parent(kid) == slot),
+            key=lambda kid: (kid[1] == slot[1], kid[0] % 2, abs(kid[0])),
+        )
+    )
     for slot in SLOTS
 }
 
@@ -56,10 +63,10 @@
 
 
 def kernel(
-    scale_hbm, bias_hbm, img_hbm, txt_hbm, gi_ref, gt_ref,
+    scale_hbm, bias_hbm, img_hbm, txt_hbm, gi_hbm, gt_hbm,
     scale, bias, img_in, txt_in, img, txt, img_acc, txt_acc,
-    y_send, y_recv, z_send, z_recv, g_send, g_recv, p_recv,
-    in_sem, ag_ss, ag_rs, t_ss, t_rs, y_ss, y_rs, z_ss, z_rs, g_ss, g_rs, p_ss, p_rs,
+    i_send, i_recv, g_send, g_recv, p_recv, gi, gt,
+    in_sem, out_sem, ag_ss, ag_rs, t_ss, t_rs, i_ss, i_rs, g_ss, g_rs, p_ss, p_rs,
 ):
     o = lax.axis_index("outer")
     i = lax.axis_index("inner")
@@ -89,7 +96,7 @@
     def greet(device):
         pl.semaphore_signal(barrier, inc=1, device_id=device, device_id_type=MESH)
 
-    peers = [along_z(0, True)] + [along_z(dz, False) for dz in (1, -1, 2, -2, 3, -3)]
+    peers = [along_z(0, True)] + [along_z(dz, False) for dz in (1, -1, 2, -2)]
     peers += [at(1 - 2 * core), at(side), at(2), at(-2)]
     for peer in peers:
         greet(peer)
@@ -128,7 +135,7 @@
 
     def gather_copy(kid):
         dz, dy = kid
-        pz, py = gather_parent(kid)
+        pz, py = tree_parent(kid)
         a, b = INDEX[(pz, py)], INDEX[kid]
         return pltpu.make_async_remote_copy(
             src_ref=img.at[a * IMG:(a + 1) * IMG],
@@ -230,25 +237,7 @@
         else:
             txt_acc[s0:s0 + n] += text_part
 
-    def y_copy(stage):
-        a, b = STAGE_AT[stage] * IMG // 2, STAGE_AT[stage + 1] * IMG // 2
-        return pltpu.make_async_remote_copy(
-            src_ref=y_send.at[a:b],
-            dst_ref=y_recv.at[a:b],
-            send_sem=y_ss.at[stage],
-            recv_sem=y_rs.at[stage],
-            device_id=along_z(0, True),
-            device_id_type=MESH,
-        )
-
-    def y_start(stage):
-        a, b = STAGE_AT[stage] * IMG // 2, STAGE_AT[stage + 1] * IMG // 2
-        y_send[a:b, :] = img_acc[a + b:2 * b, :].astype(jnp.bfloat16)
-        y_copy(stage).start()
-
-    for slot in ((2, 0), (-2, 0), (2, 1), (-2, 1)):
-        pass_on(slot)
-    for slot in ((1, 0), (-1, 0), (1, 1), (-1, 1)):
+    for slot in ((2, 0), (-2, 0), (2, 1), (-2, 1), (1, 0), (-1, 0), (1, 1), (-1, 1)):
         pass_on(slot)
     all_arrived(1)
     tile(0, 0, (0, 1), True, True)
@@ -271,18 +260,18 @@
 
         text_four[part].start()
         text_five[part].start()
+    pass_on((3, 0))
+    pass_on((-3, 0))
     tile(0, 0, (2, 3), False, True)
-    for slot in ((3, 0), (-3, 0), (3, 1), (-3, 1)):
-        pass_on(slot)
+    pass_on((5, 0))
+    pass_on((-5, 0))
+    pass_on((3, 1))
+    pass_on((-3, 1))
     tile(1, 1, (0, 1, 2, 3), True, False)
     all_arrived(4)
     all_arrived(5)
     tile(0, 1, (4, 5), False, True)
-    all_arrived(6)
-    tile(0, 1, (6,), False, True)
-    y_start(1)
-    y_start(0)
-    for slot in STAGES[2]:
+    for slot in ((6, 0), (6, 1), (5, 1), (-5, 1)):
         pass_on(slot)
 
     def grad_copy(source, slot, n, device, part):
@@ -326,56 +315,46 @@
     def pair_arrived(n):
         pair_copy(1, n).wait_recv()
 
-    def z_copy(dz):
-        n = Z_INDEX[dz]
-        hop = dz - sign(dz) * 3 if abs(dz) > 3 else dz
+    def image_copy(slot):
+        pz, py = tree_parent(slot)
+        rows = pl.ds(INDEX[slot] * IMG, IMG)
         return pltpu.make_async_remote_copy(
-            src_ref=z_send.at[n],
-            dst_ref=z_recv.at[n],
-            send_sem=z_ss.at[n],
-            recv_sem=z_rs.at[n],
-            device_id=along_z(-hop, False),
+            src_ref=i_send.at[rows],
+            dst_ref=i_recv.at[rows],
+            send_sem=i_ss.at[INDEX[slot]],
+            recv_sem=i_rs.at[INDEX[slot]],
+            device_id=along_z(pz - slot[0], py != slot[1]),
             device_id_type=MESH,
         )
 
-    def y_sum(dz):
-        stage = 0 if abs(dz) < 3 else 1 if abs(dz) < 5 else 2
-        a = INDEX[(dz, 0)] * IMG
-        b = STAGE_AT[stage] * IMG // 2 + STAGE_Z[stage].index(dz) * IMG
-        return img_acc[a:a + IMG, :] + y_recv[b:b + IMG, :].astype(jnp.float32)
-
-    def z_start(dz, total):
-        z_send[Z_INDEX[dz]] = total.astype(jnp.bfloat16)
-        z_copy(dz).start()
-
-    def z_got(dz):
-        z_copy(dz).wait_recv()
-        return z_recv[Z_INDEX[dz]].astype(jnp.float32)
-
-    tile(2, 2, (4, 5, 6), True, False)
+    def image_sum(slot):
+        total = img_acc[pl.ds(INDEX[slot] * IMG, IMG), :]
+        for kid in KIDS[slot]:
+            image_copy(kid).wait_recv()
+            total = total + i_recv[pl.ds(INDEX[kid] * IMG, IMG), :].astype(jnp.float32)
+        return total
+
+    def give_back(*slots):
+        for slot in slots:
+            i_send[pl.ds(INDEX[slot] * IMG, IMG), :] = image_sum(slot).astype(jnp.bfloat16)
+            image_copy(slot).start()
+
+    tile(2, 2, (0, 1, 2, 3, 4, 5), True, False)
     pair_early.start()
+    pair_late.start()
+    pair_own.start()
+    all_arrived(6)
+    tile(0, 2, (6,), False, True)
     g_send[2] = txt_acc[6].astype(jnp.bfloat16)
     for copy in grad_far:
         copy.start()
-    pair_late.start()
-    tile(2, 2, (0, 1, 2, 3), False, False)
-    y_start(2)
+    give_back((6, 0), (5, 1), (6, 1), (-5, 1), (4, 1), (3, 1), (-3, 1), (1, 1), (-1, 1))
     pair_arrived(1 + core)
     for part in range(PARTS):
         rows = pl.ds(part * PART, PART)
         g_send[0, rows] = (txt_acc[2 + core, rows] + p_recv[1 + core, rows]).astype(jnp.bfloat16)
         grad_early[part].start()
-    pair_own.start()
-
-    y_copy(1).wait_recv()
-    for dz in (4, -4):
-        z_start(dz, y_sum(dz))
-    y_copy(0).wait_recv()
-    for dz in (2, -2, 1, -1):
-        z_start(dz, y_sum(dz))
-    y_copy(2).wait_recv()
-    for dz in (6, 5, -5):
-        z_start(dz, y_sum(dz))
+    give_back((5, 0), (-5, 0), (3, 0), (-3, 0), (4, 0), (-4, 1), (-4, 0))
 
     pair_arrived(2 - core)
     for part in range(PARTS):
@@ -394,6 +373,8 @@
 
         grad_late[part].start()
 
+    give_back((1, 0), (-1, 0))
+
     @pl.when(outer_end == 1)
     def _():
         for part in range(PARTS):
@@ -412,18 +393,20 @@
     def _():
         go_through()
 
-    z_start(3, y_sum(3) + z_got(4) + z_got(5) + z_got(6))
-    z_start(-3, y_sum(-3) + z_got(-4) + z_got(-5))
+    give_back((2, 1), (-2, 1), (2, 0), (-2, 0), (0, 1))
 
     @pl.when(late_through == 1)
     def _():
         go_through()
 
     inverse, full = unit_rows(img_in[...])
-    image_total = y_sum(0)
-    for dz in (1, -1, 2, -2, 3, -3):
-        image_total = image_total + z_got(dz)
-    gi_ref[...] = project_back(inverse, full, image_total * factor)
+    gi[...] = project_back(inverse, full, image_sum((0, 0)) * factor)
+    store_img = pltpu.make_async_copy(gi, gi_hbm, out_sem.at[0])
+    store_img.start()
+
+    def store_txt(part):
+        rows = pl.ds(part * PART, PART)
+        return pltpu.make_async_copy(gt.at[rows], gt_hbm.at[rows], out_sem.at[1 + part])
 
     pair_arrived(0)
     for part in range(PARTS):
@@ -440,13 +423,13 @@
             txt_acc[0, rows] += g_recv[5, rows].astype(jnp.float32)
 
         inverse, full = unit_rows(txt_in[rows, :])
-        gt_ref[rows, :] = project_back(inverse, full, txt_acc[0, rows] * factor)
+        gt[rows, :] = project_back(inverse, full, txt_acc[0, rows] * factor)
+        store_txt(part).start()
 
     for slot in SLOTS[1:]:
         gather_copy(slot).wait_send()
-    for dz in Z_SLOTS:
-        z_copy(dz).wait_send()
-    for copy in (y_copy(0), y_copy(1), y_copy(2), pair_own, pair_early, pair_late):
+        image_copy(slot).wait_send()
+    for copy in (pair_own, pair_early, pair_late):
         copy.wait_send()
     for copies in (text_partner, text_up, text_down, text_four, text_five, grad_far, grad_early, grad_late):
         for copy in copies:
@@ -466,6 +449,10 @@
     def _():
         for copy in text_through + grad_through:
             copy.wait_send()
+
+    store_img.wait()
+    for part in range(PARTS):
+        store_txt(part).wait()
 
 
 def local(images, texts, logit_scale, logit_bias):
@@ -478,7 +465,7 @@
             jax.ShapeDtypeStruct((TXT, D), f32),
         ),
         in_specs=[pl.BlockSpec(memory_space=pl.ANY)] * 4,
-        out_specs=[pl.BlockSpec(memory_space=pltpu.VMEM)] * 2,
+        out_specs=[pl.BlockSpec(memory_space=pl.ANY)] * 2,
         scratch_shapes=[
             pltpu.SMEM((1,), f32),
             pltpu.SMEM((1,), f32),
@@ -488,18 +475,17 @@
             pltpu.VMEM((9, TXT, D), bf),
             pltpu.VMEM((NI * IMG, D), f32),
             pltpu.VMEM((7, TXT, D), f32),
-            pltpu.VMEM((NI * IMG // 2, D), bf),
-            pltpu.VMEM((NI * IMG // 2, D), bf),
-            pltpu.VMEM((11, IMG, D), bf),
-            pltpu.VMEM((11, IMG, D), bf),
+            pltpu.VMEM((NI * IMG, D), bf),
+            pltpu.VMEM((NI * IMG, D), bf),
             pltpu.VMEM((3, TXT, D), bf),
             pltpu.VMEM((7, TXT, D), bf),
             pltpu.VMEM((3, TXT, D), f32),
-            dma((4,)),
+            pltpu.VMEM((IMG, D), f32),
+            pltpu.VMEM((TXT, D), f32),
+            dma((4,)), dma((1 + PARTS,)),
             dma((NI,)), dma((NI,)),
             dma((8, PARTS)), dma((9, PARTS)),
-            dma((3,)), dma((3,)),
-            dma((11,)), dma((11,)),
+            dma((NI,)), dma((NI,)),
             dma((5, PARTS)), dma((7, PARTS)),
             dma((3,)), dma((3,)),
         ],

time: 71.9 us -> 93.6 us (1.30)
  the two profiles are of different devices: /device:TPU:64 before, /device:TPU:40 now
where the time goes in v3:
time: 93.6 us; the launch traced here: 93.4 us
  Pallas kernels  88.3 us (94%)
  local copies, waits for them, and re-layouts  3.17 us (3%)
  between operations  1.94 us (2%)
    pallas_call x1, Pallas kernels, local(): pl.pallas_call(kernel, out_shape=(jax.ShapeDtypeStruct((IMG, D), f32), ja...  88.3 us
    unnamed x6, local copies, waits for them, and re-layouts  3.17 us

profile of v3, /device:TPU:40, one launch (start us, length us, event | category | flops | bytes accessed | tf_op | source)
XLA Modules:
  0.0 93.4 jit_solution(9489392455458960245)
XLA Ops:
  1.9 0.0 copy-start
  1.9 1.0 %copy-done = bf16[128,1152]{1,0:T(8,128)(2,1)S(1)} copy-done((bf16[128,1152]{1,0:T(8,128)(2,1)S(1)}, bf16[128,1152]{1,0:T(8,128)(2,1)}, u32[]{:S(2)}) %copy-start) | copy-done | bytes 294936
  2.9 0.0 copy-start.1
  2.9 0.8 copy-done.1
  3.7 88.3 %pair_gradients.1 = (f32[16,1152]{1,0:T(8,128)S(1)}, f32[128,1152]{1,0:T(8,128)S(1)}) custom-call(f32[1]{0:T(128)S(6)} %copy.8.scale_hbm, f32[1]{0:T(128)S(6)} %copy.9.bias_hbm, bf16[16,1152]{1,0:T(8,128)(2,1)S(1)} %copy-done.1, bf16[128,1152]{1,0:T(8,128)(2,1)S(1)} %copy-done), custom_call_target="tpu_custom_call" | custom-call | tf_op jit(solution)/shard_map/pair_gradients/pallas_call | solution.py:461
  91.9 0.6 copy.10
  92.6 0.8 copy.11
Async XLA Ops:
  1.9 1.0 %copy-start = (bf16[128,1152]{1,0:T(8,128)(2,1)S(1)}, bf16[128,1152]{1,0:T(8,128)(2,1)}, u32[]{:S(2)}) copy-start(bf16[128,1152]{1,0:T(8,128)(2,1)} %txt_hbm.1) | copy-start | bytes 884740
  2.9 0.8 copy-start.1

commit v4 on v3

--- a/solution.py
+++ b/solution.py
@@ -29,26 +29,48 @@
     return (value > 0) - (value < 0)
 
 
-def tree_parent(slot):
+def gather_parent(slot):
+    dz, dy = slot
+    if dz == 0:
+        return (0, 0)
+    if dz == 6:
+        return (4, 0) if dy == 0 else (-4, 1)
+    if dz in (2, -2):
+        return (0, 0)
+    return (sign(dz) * ((abs(dz) - 1) // 2 * 2), dy)
+
+
+def return_parent(slot):
     dz, dy = slot
     if dz == 6:
-        return (4, 0) if dy == 0 else (-4, 1)
-    if dz == 0:
-        return (0, 0)
-    if dz % 2 == 0:
-        return (dz - 2 * sign(dz), dy)
-    return (dz, 0) if dy else (dz - sign(dz), 0)
-
-
-KIDS = {
-    slot: tuple(
-        sorted(
-            (kid for kid in SLOTS if kid != (0, 0) and tree_parent(kid) == slot),
-            key=lambda kid: (kid[1] == slot[1], kid[0] % 2, abs(kid[0])),
-        )
-    )
-    for slot in SLOTS
-}
+        return (3, 0) if dy == 0 else (-3, 0)
+    if dy and abs(dz) < 5:
+        return (dz, 0)
+    return (sign(dz) * ((abs(dz) - 1) // 3 * 3), 0)
+
+
+def kids_of(parent):
+    return {
+        slot: tuple(
+            sorted((kid for kid in SLOTS[1:] if parent(kid) == slot), key=lambda kid: (kid[1] == slot[1], -abs(kid[0])))
+        )
+        for slot in SLOTS
+    }
+
+
+def move(start, end):
+    dz = (end[0] - start[0]) % NZ
+    return (dz - NZ if dz > NZ // 2 else dz, (end[1] - start[1]) % 2)
+
+
+GATHER_KIDS = kids_of(gather_parent)
+RETURN_KIDS = kids_of(return_parent)
+MOVES = sorted(
+    {move(gather_parent(slot), slot) for slot in SLOTS[1:]}
+    | {move(slot, gather_parent(slot)) for slot in SLOTS[1:]}
+    | {move(slot, return_parent(slot)) for slot in SLOTS[1:]}
+    | {move(return_parent(slot), slot) for slot in SLOTS[1:]}
+)
 
 
 def unit_rows(values):
@@ -65,7 +87,7 @@
 def kernel(
     scale_hbm, bias_hbm, img_hbm, txt_hbm, gi_hbm, gt_hbm,
     scale, bias, img_in, txt_in, img, txt, img_acc, txt_acc,
-    i_send, i_recv, g_send, g_recv, p_recv, gi, gt,
+    i_send, i_recv, g_send, g_recv, p_send, p_recv, gi, gt,
     in_sem, out_sem, ag_ss, ag_rs, t_ss, t_rs, i_ss, i_rs, g_ss, g_rs, p_ss, p_rs,
 ):
     o = lax.axis_index("outer")
@@ -96,7 +118,7 @@
     def greet(device):
         pl.semaphore_signal(barrier, inc=1, device_id=device, device_id_type=MESH)
 
-    peers = [along_z(0, True)] + [along_z(dz, False) for dz in (1, -1, 2, -2)]
+    peers = [along_z(dz, flip) for dz, flip in MOVES]
     peers += [at(1 - 2 * core), at(side), at(2), at(-2)]
     for peer in peers:
         greet(peer)
@@ -134,22 +156,21 @@
     pl.semaphore_wait(barrier, len(peers) + 3 * through + 2 * inner_end + 4 * outer_end)
 
     def gather_copy(kid):
-        dz, dy = kid
-        pz, py = tree_parent(kid)
-        a, b = INDEX[(pz, py)], INDEX[kid]
+        parent = gather_parent(kid)
+        a, b = INDEX[parent], INDEX[kid]
         return pltpu.make_async_remote_copy(
             src_ref=img.at[a * IMG:(a + 1) * IMG],
             dst_ref=img.at[b * IMG:(b + 1) * IMG],
             send_sem=ag_ss.at[b],
             recv_sem=ag_rs.at[b],
-            device_id=along_z(dz - pz, dy != py),
+            device_id=along_z(*move(parent, kid)),
             device_id_type=MESH,
         )
 
     def pass_on(slot):
         if slot != (0, 0):
             gather_copy(slot).wait_recv()
-        for kid in KIDS[slot]:
+        for kid in GATHER_KIDS[slot]:
             gather_copy(kid).start()
 
     def text_copy(source, slot, n, device, part):
@@ -237,42 +258,73 @@
         else:
             txt_acc[s0:s0 + n] += text_part
 
-    for slot in ((2, 0), (-2, 0), (2, 1), (-2, 1), (1, 0), (-1, 0), (1, 1), (-1, 1)):
+    ahead = 1 - z // (NZ // 2)
+    plus = ((z + 9) % NZ) // (NZ // 2)
+
+    def pass_side(plus_side, *places):
+        for value, side_sign in ((plus_side, 1), (1 - plus_side, -1)):
+
+            @pl.when(value == 1)
+            def _():
+                for dz in places:
+                    pass_on((side_sign * dz, 0))
+                    pass_on((side_sign * dz, 1))
+
+    def relay_texts():
+        @pl.when(through == 1)
+        def _():
+            for part in range(PARTS):
+                text_arrived(7 + last, part)
+                text_through[part].start()
+
+    def pass_texts():
+        for part in range(PARTS):
+            text_arrived(2, part)
+            text_arrived(3, part)
+
+            @pl.when(inner_end == 0)
+            def _():
+                text_far[part].start()
+
+            text_four[part].start()
+            text_five[part].start()
+
+    @pl.when(ahead == 1)
+    def _():
+        relay_texts()
+        pass_texts()
+
+    pass_side(1 - plus, 2)
+    pass_side(plus, 2)
+    pass_side(1 - plus, 4)
+
+    @pl.when(ahead == 1)
+    def _():
+        pass_side(plus, 4)
+
+    @pl.when(ahead == 0)
+    def _():
+        relay_texts()
+
+    for slot in ((1, 0), (-1, 0), (1, 1), (-1, 1)):
         pass_on(slot)
     all_arrived(1)
     tile(0, 0, (0, 1), True, True)
 
-    @pl.when(through == 1)
-    def _():
-        for part in range(PARTS):
-            text_arrived(7 + last, part)
-            text_through[part].start()
-
-    for slot in ((4, 0), (-4, 0), (4, 1), (-4, 1)):
+    @pl.when(ahead == 0)
+    def _():
+        pass_side(plus, 4)
+        pass_texts()
+
+    tile(0, 0, (2, 3), False, True)
+    for slot in ((3, 0), (-3, 0), (3, 1), (-3, 1)):
         pass_on(slot)
-    for part in range(PARTS):
-        text_arrived(2, part)
-        text_arrived(3, part)
-
-        @pl.when(inner_end == 0)
-        def _():
-            text_far[part].start()
-
-        text_four[part].start()
-        text_five[part].start()
-    pass_on((3, 0))
-    pass_on((-3, 0))
-    tile(0, 0, (2, 3), False, True)
-    pass_on((5, 0))
-    pass_on((-5, 0))
-    pass_on((3, 1))
-    pass_on((-3, 1))
     tile(1, 1, (0, 1, 2, 3), True, False)
     all_arrived(4)
     all_arrived(5)
     tile(0, 1, (4, 5), False, True)
-    for slot in ((6, 0), (6, 1), (5, 1), (-5, 1)):
-        pass_on(slot)
+    all_arrived(6)
+    tile(0, 1, (6,), False, True)
 
     def grad_copy(source, slot, n, device, part):
         return pltpu.make_async_remote_copy(
@@ -287,9 +339,9 @@
     def grad_copies(source, slot, n, device):
         return [grad_copy(source, slot, n, device, part) for part in range(PARTS)]
 
-    def pair_copy(slot, n):
+    def pair_copy(n):
         return pltpu.make_async_remote_copy(
-            src_ref=txt_acc.at[slot],
+            src_ref=p_send.at[n],
             dst_ref=p_recv.at[n],
             send_sem=p_ss.at[n],
             recv_sem=p_rs.at[n],
@@ -307,29 +359,28 @@
     grad_late = grad_copies(g_send.at[1], late_slot, 1, at(late_shift))
     grad_through = grad_copies(g_recv.at[3 + last], last, 3, at(8 * first - 8 * last))
     grad_far_through = grad_copies(g_recv.at[6], 5, 4, at(-8 * side))
-    pair_own, pair_early, pair_late = pair_copy(1, 0), pair_copy(5 - core, 2 - core), pair_copy(4 + core, 1 + core)
+    pair_own, pair_early, pair_late = pair_copy(0), pair_copy(2 - core), pair_copy(1 + core)
 
     def grad_arrived(slot, part):
         grad_copy(g_send.at[0], slot, 0, partner, part).wait_recv()
 
     def pair_arrived(n):
-        pair_copy(1, n).wait_recv()
+        pair_copy(n).wait_recv()
 
     def image_copy(slot):
-        pz, py = tree_parent(slot)
         rows = pl.ds(INDEX[slot] * IMG, IMG)
         return pltpu.make_async_remote_copy(
             src_ref=i_send.at[rows],
             dst_ref=i_recv.at[rows],
             send_sem=i_ss.at[INDEX[slot]],
             recv_sem=i_rs.at[INDEX[slot]],
-            device_id=along_z(pz - slot[0], py != slot[1]),
+            device_id=along_z(*move(slot, return_parent(slot))),
             device_id_type=MESH,
         )
 
     def image_sum(slot):
         total = img_acc[pl.ds(INDEX[slot] * IMG, IMG), :]
-        for kid in KIDS[slot]:
+        for kid in RETURN_KIDS[slot]:
             image_copy(kid).wait_recv()
             total = total + i_recv[pl.ds(INDEX[kid] * IMG, IMG), :].astype(jnp.float32)
         return total
@@ -339,22 +390,27 @@
             i_send[pl.ds(INDEX[slot] * IMG, IMG), :] = image_sum(slot).astype(jnp.bfloat16)
             image_copy(slot).start()
 
-    tile(2, 2, (0, 1, 2, 3, 4, 5), True, False)
-    pair_early.start()
-    pair_late.start()
-    pair_own.start()
-    all_arrived(6)
-    tile(0, 2, (6,), False, True)
+    give_back((0, 1), (4, 1), (-4, 1), (3, 1), (-3, 1), (2, 1), (-2, 1), (1, 1), (-1, 1))
+    for slot in STAGES[2]:
+        pass_on(slot)
+    tile(2, 2, (4, 5, 6), True, False)
     g_send[2] = txt_acc[6].astype(jnp.bfloat16)
     for copy in grad_far:
         copy.start()
-    give_back((6, 0), (5, 1), (6, 1), (-5, 1), (4, 1), (3, 1), (-3, 1), (1, 1), (-1, 1))
+    p_send[2 - core] = txt_acc[5 - core].astype(jnp.bfloat16)
+    pair_early.start()
+    p_send[1 + core] = txt_acc[4 + core].astype(jnp.bfloat16)
+    pair_late.start()
+    tile(2, 2, (0, 1, 2, 3), False, False)
+    give_back((6, 0), (6, 1), (5, 1), (-5, 1), (5, 0), (-5, 0), (4, 0), (-4, 0))
     pair_arrived(1 + core)
     for part in range(PARTS):
         rows = pl.ds(part * PART, PART)
-        g_send[0, rows] = (txt_acc[2 + core, rows] + p_recv[1 + core, rows]).astype(jnp.bfloat16)
+        g_send[0, rows] = (txt_acc[2 + core, rows] + p_recv[1 + core, rows].astype(jnp.float32)).astype(jnp.bfloat16)
         grad_early[part].start()
-    give_back((5, 0), (-5, 0), (3, 0), (-3, 0), (4, 0), (-4, 1), (-4, 0))
+    p_send[0] = txt_acc[1].astype(jnp.bfloat16)
+    pair_own.start()
+    give_back((2, 0), (-2, 0), (1, 0), (-1, 0))
 
     pair_arrived(2 - core)
     for part in range(PARTS):
@@ -364,16 +420,20 @@
         def _():
             grad_arrived(2, part)
             g_send[1, rows] = (
-                txt_acc[3 - core, rows] + p_recv[2 - core, rows] + g_recv[2, rows].astype(jnp.float32)
+                txt_acc[3 - core, rows]
+                + p_recv[2 - core, rows].astype(jnp.float32)
+                + g_recv[2, rows].astype(jnp.float32)
             ).astype(jnp.bfloat16)
 
         @pl.when(inner_end == 1)
         def _():
-            g_send[1, rows] = (txt_acc[3 - core, rows] + p_recv[2 - core, rows]).astype(jnp.bfloat16)
+            g_send[1, rows] = (
+                txt_acc[3 - core, rows] + p_recv[2 - core, rows].astype(jnp.float32)
+            ).astype(jnp.bfloat16)
 
         grad_late[part].start()
 
-    give_back((1, 0), (-1, 0))
+    give_back((3, 0), (-3, 0))
 
     @pl.when(outer_end == 1)
     def _():
@@ -393,7 +453,6 @@
     def _():
         go_through()
 
-    give_back((2, 1), (-2, 1), (2, 0), (-2, 0), (0, 1))
 
     @pl.when(late_through == 1)
     def _():
@@ -413,7 +472,7 @@
         rows = pl.ds(part * PART, PART)
         grad_arrived(0, part)
         grad_arrived(1, part)
-        txt_acc[0, rows] += p_recv[0, rows] + (
+        txt_acc[0, rows] += p_recv[0, rows].astype(jnp.float32) + (
             g_recv[0, rows].astype(jnp.float32) + g_recv[1, rows].astype(jnp.float32)
         )
 
@@ -479,7 +538,8 @@
             pltpu.VMEM((NI * IMG, D), bf),
             pltpu.VMEM((3, TXT, D), bf),
             pltpu.VMEM((7, TXT, D), bf),
-            pltpu.VMEM((3, TXT, D), f32),
+            pltpu.VMEM((3, TXT, D), bf),
+            pltpu.VMEM((3, TXT, D), bf),
             pltpu.VMEM((IMG, D), f32),
             pltpu.VMEM((TXT, D), f32),
             dma((4,)), dma((1 + PARTS,)),

time: 93.6 us -> 80.1 us (0.86)
  the two profiles are of different devices: /device:TPU:40 before, /device:TPU:8 now
where the time goes in v4:
time: 80.1 us; the launch traced here: 79.8 us
  Pallas kernels  74.7 us (93%)
  local copies, waits for them, and re-layouts  3.17 us (4%)
  between operations  1.94 us (2%)
    pallas_call x1, Pallas kernels, local(): pl.pallas_call(kernel, out_shape=(jax.ShapeDtypeStruct((IMG, D), f32), ja...  74.7 us
    unnamed x6, local copies, waits for them, and re-layouts  3.17 us

profile of v4, /device:TPU:8, one launch (start us, length us, event | category | flops | bytes accessed | tf_op | source)
XLA Modules:
  0.0 79.8 jit_solution(17280930583416312851)
XLA Ops:
  1.9 0.0 copy-start
  1.9 1.0 %copy-done = bf16[128,1152]{1,0:T(8,128)(2,1)S(1)} copy-done((bf16[128,1152]{1,0:T(8,128)(2,1)S(1)}, bf16[128,1152]{1,0:T(8,128)(2,1)}, u32[]{:S(2)}) %copy-start) | copy-done | bytes 294936
  2.9 0.0 copy-start.1
  2.9 0.8 copy-done.1
  3.7 74.7 %pair_gradients.1 = (f32[16,1152]{1,0:T(8,128)S(1)}, f32[128,1152]{1,0:T(8,128)S(1)}) custom-call(f32[1]{0:T(128)S(6)} %copy.8.scale_hbm, f32[1]{0:T(128)S(6)} %copy.9.bias_hbm, bf16[16,1152]{1,0:T(8,128)(2,1)S(1)} %copy-done.1, bf16[128,1152]{1,0:T(8,128)(2,1)S(1)} %copy-done), custom_call_target="tpu_custom_call" | custom-call | tf_op jit(solution)/shard_map/pair_gradients/pallas_call | solution.py:520
  78.4 0.6 copy.10
  79.0 0.8 %copy.11 = f32[128,1152]{1,0:T(8,128)} copy(f32[128,1152]{1,0:T(8,128)S(1)} %get-tuple-element.5) | data formatting | bytes 1179648
Async XLA Ops:
  1.9 1.0 %copy-start = (bf16[128,1152]{1,0:T(8,128)(2,1)S(1)}, bf16[128,1152]{1,0:T(8,128)(2,1)}, u32[]{:S(2)}) copy-start(bf16[128,1152]{1,0:T(8,128)(2,1)} %txt_hbm.1) | copy-start | bytes 884740
  2.9 0.8 copy-start.1

commit v5 on v4

--- a/solution.py
+++ b/solution.py
@@ -258,64 +258,31 @@
         else:
             txt_acc[s0:s0 + n] += text_part
 
-    ahead = 1 - z // (NZ // 2)
-    plus = ((z + 9) % NZ) // (NZ // 2)
-
-    def pass_side(plus_side, *places):
-        for value, side_sign in ((plus_side, 1), (1 - plus_side, -1)):
-
-            @pl.when(value == 1)
-            def _():
-                for dz in places:
-                    pass_on((side_sign * dz, 0))
-                    pass_on((side_sign * dz, 1))
-
-    def relay_texts():
-        @pl.when(through == 1)
-        def _():
-            for part in range(PARTS):
-                text_arrived(7 + last, part)
-                text_through[part].start()
-
-    def pass_texts():
+    for slot in ((2, 0), (-2, 0), (2, 1), (-2, 1)):
+        pass_on(slot)
+
+    @pl.when(through == 1)
+    def _():
         for part in range(PARTS):
-            text_arrived(2, part)
-            text_arrived(3, part)
-
-            @pl.when(inner_end == 0)
-            def _():
-                text_far[part].start()
-
-            text_four[part].start()
-            text_five[part].start()
-
-    @pl.when(ahead == 1)
-    def _():
-        relay_texts()
-        pass_texts()
-
-    pass_side(1 - plus, 2)
-    pass_side(plus, 2)
-    pass_side(1 - plus, 4)
-
-    @pl.when(ahead == 1)
-    def _():
-        pass_side(plus, 4)
-
-    @pl.when(ahead == 0)
-    def _():
-        relay_texts()
+            text_arrived(7 + last, part)
+            text_through[part].start()
 
     for slot in ((1, 0), (-1, 0), (1, 1), (-1, 1)):
         pass_on(slot)
     all_arrived(1)
     tile(0, 0, (0, 1), True, True)
-
-    @pl.when(ahead == 0)
-    def _():
-        pass_side(plus, 4)
-        pass_texts()
-
+    for slot in ((4, 0), (-4, 0), (4, 1), (-4, 1)):
+        pass_on(slot)
+    for part in range(PARTS):
+        text_arrived(2, part)
+        text_arrived(3, part)
+
+        @pl.when(inner_end == 0)
+        def _():
+            text_far[part].start()
+
+        text_four[part].start()
+        text_five[part].start()
     tile(0, 0, (2, 3), False, True)
     for slot in ((3, 0), (-3, 0), (3, 1), (-3, 1)):
         pass_on(slot)

time: 80.1 us -> 68.4 us (0.85)
  the two profiles are of different devices: /device:TPU:8 before, /device:TPU:2 now
where the time goes in v5:
time: 68.4 us; the launch traced here: 68.2 us
  Pallas kernels  63.1 us (92%)
  local copies, waits for them, and re-layouts  3.17 us (5%)
  between operations  1.94 us (3%)
    pallas_call x1, Pallas kernels, local(): pl.pallas_call(kernel, out_shape=(jax.ShapeDtypeStruct((IMG, D), f32), ja...  63.1 us
    unnamed x6, local copies, waits for them, and re-layouts  3.17 us

profile of v5, /device:TPU:2, one launch (start us, length us, event | category | flops | bytes accessed | tf_op | source)
XLA Modules:
  0.0 68.2 jit_solution(300524874608222890)
XLA Ops:
  1.9 0.0 copy-start
  1.9 1.0 %copy-done = bf16[128,1152]{1,0:T(8,128)(2,1)S(1)} copy-done((bf16[128,1152]{1,0:T(8,128)(2,1)S(1)}, bf16[128,1152]{1,0:T(8,128)(2,1)}, u32[]{:S(2)}) %copy-start) | copy-done | bytes 294936
  2.9 0.0 copy-start.1
  2.9 0.8 %copy-done.1 = bf16[16,1152]{1,0:T(8,128)(2,1)S(1)} copy-done((bf16[16,1152]{1,0:T(8,128)(2,1)S(1)}, bf16[16,1152]{1,0:T(8,128)(2,1)}, u32[]{:S(2)}) %copy-start.1) | copy-done | bytes 36888
  3.7 63.1 %pair_gradients.1 = (f32[16,1152]{1,0:T(8,128)S(1)}, f32[128,1152]{1,0:T(8,128)S(1)}) custom-call(f32[1]{0:T(128)S(6)} %copy.8.scale_hbm, f32[1]{0:T(128)S(6)} %copy.9.bias_hbm, bf16[16,1152]{1,0:T(8,128)(2,1)S(1)} %copy-done.1, bf16[128,1152]{1,0:T(8,128)(2,1)S(1)} %copy-done), custom_call_target="tpu_custom_call" | custom-call | tf_op jit(solution)/shard_map/pair_gradients/pallas_call | solution.py:487
  66.7 0.6 copy.10
  67.4 0.8 %copy.11 = f32[128,1152]{1,0:T(8,128)} copy(f32[128,1152]{1,0:T(8,128)S(1)} %get-tuple-element.5) | data formatting | bytes 1179648
Async XLA Ops:
  1.9 1.0 %copy-start = (bf16[128,1152]{1,0:T(8,128)(2,1)S(1)}, bf16[128,1152]{1,0:T(8,128)(2,1)}, u32[]{:S(2)}) copy-start(bf16[128,1152]{1,0:T(8,128)(2,1)} %txt_hbm.1) | copy-start | bytes 884740
  2.9 0.8 %copy-start.1 = (bf16[16,1152]{1,0:T(8,128)(2,1)S(1)}, bf16[16,1152]{1,0:T(8,128)(2,1)}, u32[]{:S(2)}) copy-start(bf16[16,1152]{1,0:T(8,128)(2,1)} %img_hbm.1) | copy-start | bytes 110596

commit v6 on v5

--- a/solution.py
+++ b/solution.py
@@ -21,7 +21,9 @@
 SLOTS = tuple(slot for stage in STAGES for slot in stage)
 INDEX = {slot: n for n, slot in enumerate(SLOTS)}
 STAGE_AT = (0, 10, 18, 24)
+LATE_SLOTS = ((3, 0), (-3, 0))
 PARTS = 4
+HALVES = 2
 PART = TXT // PARTS
 
 
@@ -68,8 +70,6 @@
 MOVES = sorted(
     {move(gather_parent(slot), slot) for slot in SLOTS[1:]}
     | {move(slot, gather_parent(slot)) for slot in SLOTS[1:]}
-    | {move(slot, return_parent(slot)) for slot in SLOTS[1:]}
-    | {move(return_parent(slot), slot) for slot in SLOTS[1:]}
 )
 
 
@@ -87,7 +87,7 @@
 def kernel(
     scale_hbm, bias_hbm, img_hbm, txt_hbm, gi_hbm, gt_hbm,
     scale, bias, img_in, txt_in, img, txt, img_acc, txt_acc,
-    i_send, i_recv, g_send, g_recv, p_send, p_recv, gi, gt,
+    i_send, i_recv, g_send, g_recv, p_send, p_recv, gi, gt, inv_img, inv_txt,
     in_sem, out_sem, ag_ss, ag_rs, t_ss, t_rs, i_ss, i_rs, g_ss, g_rs, p_ss, p_rs,
 ):
     o = lax.axis_index("outer")
@@ -113,6 +113,15 @@
     outer_end = (x // 2) * (1 - x % 2) * core + (x % 2) * (1 - x // 2) * (1 - core)
     side = 2 * core - 1
 
+    loads = [
+        pltpu.make_async_copy(source, target, in_sem.at[n])
+        for n, (source, target) in enumerate(
+            ((img_hbm, img_in), (txt_hbm, txt_in), (scale_hbm, scale), (bias_hbm, bias))
+        )
+    ]
+    for load in loads:
+        load.start()
+
     barrier = pltpu.get_barrier_semaphore()
 
     def greet(device):
@@ -141,17 +150,10 @@
         greet(at(8))
         greet(at(-8))
 
-    loads = [
-        pltpu.make_async_copy(source, target, in_sem.at[n])
-        for n, (source, target) in enumerate(
-            ((img_hbm, img_in), (txt_hbm, txt_in), (scale_hbm, scale), (bias_hbm, bias))
-        )
-    ]
-    for load in loads:
-        load.start()
     loads[0].wait()
-    _, full = unit_rows(img_in[...])
+    inv_img[...], full = unit_rows(img_in[...])
     img[0:IMG, :] = full.astype(jnp.bfloat16)
+    gi[...] = full
 
     pl.semaphore_wait(barrier, len(peers) + 3 * through + 2 * inner_end + 4 * outer_end)
 
@@ -173,8 +175,8 @@
         for kid in GATHER_KIDS[slot]:
             gather_copy(kid).start()
 
-    def text_copy(source, slot, n, device, part):
-        rows = pl.ds(part * PART, PART)
+    def text_copy(source, slot, n, device, part, parts):
+        rows = pl.ds(part * (TXT // parts), TXT // parts)
         return pltpu.make_async_remote_copy(
             src_ref=txt.at[source, rows],
             dst_ref=txt.at[slot, rows],
@@ -184,43 +186,43 @@
             device_id_type=MESH,
         )
 
-    def text_copies(source, slot, n, device):
-        return [text_copy(source, slot, n, device, part) for part in range(PARTS)]
+    def text_copies(source, slot, n, device, parts):
+        return [text_copy(source, slot, n, device, part, parts) for part in range(parts)]
 
     partner = at(1 - 2 * core)
     up = at(2 - 8 * last)
     down = at(8 * first - 2)
-    text_partner = text_copies(0, 1, 1, partner)
-    text_up = text_copies(0, 2 + 5 * last, 2, up)
-    text_down = text_copies(0, 3 + 5 * first, 3, down)
-    text_four = text_copies(2, 4, 4, partner)
-    text_five = text_copies(3, 5, 5, partner)
-    text_far = text_copies(3 - core, 6, 6, at(side))
-    text_far_own = text_copies(0, 6, 0, at(3 * side))
-    text_through = text_copies(7 + last, 2 + last, 7, at(8 * first - 8 * last))
-
-    def text_arrived(slot, part):
-        text_copy(0, slot, 0, partner, part).wait_recv()
-
-    def all_arrived(slot):
-        for part in range(PARTS):
-            text_arrived(slot, part)
+    text_partner = text_copies(0, 1, 1, partner, 1)
+    text_up = text_copies(0, 2 + 5 * last, 2, up, PARTS)
+    text_down = text_copies(0, 3 + 5 * first, 3, down, PARTS)
+    text_four = text_copies(2, 4, 4, partner, HALVES)
+    text_five = text_copies(3, 5, 5, partner, HALVES)
+    text_far = text_copies(3 - core, 6, 6, at(side), HALVES)
+    text_far_own = text_copies(0, 6, 0, at(3 * side), HALVES)
+    text_through = text_copies(7 + last, 2 + last, 7, at(8 * first - 8 * last), PARTS)
+
+    def text_arrived(slot, part, parts):
+        text_copy(0, slot, 0, partner, part, parts).wait_recv()
+
+    def all_arrived(slot, parts):
+        for part in range(parts):
+            text_arrived(slot, part, parts)
 
     pass_on((0, 0))
     loads[1].wait()
-    _, full = unit_rows(txt_in[...])
+    inv_txt[...], full = unit_rows(txt_in[...])
     txt[0] = full.astype(jnp.bfloat16)
+    gt[...] = full
     for part in range(PARTS):
         text_up[part].start()
         text_down[part].start()
 
     @pl.when(outer_end == 1)
     def _():
-        for part in range(PARTS):
+        for part in range(HALVES):
             text_far_own[part].start()
 
-    for part in range(PARTS):
-        text_partner[part].start()
+    text_partner[0].start()
     pass_on((0, 1))
     loads[2].wait()
     loads[3].wait()
@@ -264,47 +266,48 @@
     @pl.when(through == 1)
     def _():
         for part in range(PARTS):
-            text_arrived(7 + last, part)
+            text_arrived(7 + last, part, PARTS)
             text_through[part].start()
 
     for slot in ((1, 0), (-1, 0), (1, 1), (-1, 1)):
         pass_on(slot)
-    all_arrived(1)
+    all_arrived(1, 1)
     tile(0, 0, (0, 1), True, True)
     for slot in ((4, 0), (-4, 0), (4, 1), (-4, 1)):
         pass_on(slot)
-    for part in range(PARTS):
-        text_arrived(2, part)
-        text_arrived(3, part)
+    for half in range(HALVES):
+        for part in range(half * PARTS // HALVES, (half + 1) * PARTS // HALVES):
+            text_arrived(2, part, PARTS)
+            text_arrived(3, part, PARTS)
 
         @pl.when(inner_end == 0)
         def _():
-            text_far[part].start()
-
-        text_four[part].start()
-        text_five[part].start()
+            text_far[half].start()
+
+        text_four[half].start()
+        text_five[half].start()
     tile(0, 0, (2, 3), False, True)
     for slot in ((3, 0), (-3, 0), (3, 1), (-3, 1)):
         pass_on(slot)
     tile(1, 1, (0, 1, 2, 3), True, False)
-    all_arrived(4)
-    all_arrived(5)
-    tile(0, 1, (4, 5), False, True)
-    all_arrived(6)
-    tile(0, 1, (6,), False, True)
-
-    def grad_copy(source, slot, n, device, part):
+    all_arrived(4, HALVES)
+    all_arrived(5, HALVES)
+    all_arrived(6, HALVES)
+    tile(0, 1, (4, 5, 6), False, True)
+
+    def grad_copy(source, slot, n, device, part, parts):
+        rows = pl.ds(part * (TXT // parts), TXT // parts)
         return pltpu.make_async_remote_copy(
-            src_ref=source.at[pl.ds(part * PART, PART)],
-            dst_ref=g_recv.at[slot, pl.ds(part * PART, PART)],
+            src_ref=source.at[rows],
+            dst_ref=g_recv.at[slot, rows],
             send_sem=g_ss.at[n, part],
             recv_sem=g_rs.at[slot, part],
             device_id=device,
             device_id_type=MESH,
         )
 
-    def grad_copies(source, slot, n, device):
-        return [grad_copy(source, slot, n, device, part) for part in range(PARTS)]
+    def grad_copies(source, slot, n, device, parts):
+        return [grad_copy(source, slot, n, device, part, parts) for part in range(parts)]
 
     def pair_copy(n):
         return pltpu.make_async_remote_copy(
@@ -321,15 +324,15 @@
     late_shift = (1 - core) * (2 - 8 * last) + core * (8 * first - 2)
     early_slot = core * 3 * last + (1 - core) * (1 + 3 * first)
     late_slot = (1 - core) * 3 * last + core * (1 + 3 * first)
-    grad_far = grad_copies(g_send.at[2], 2 + 4 * inner_end, 2, at(far_shift))
-    grad_early = grad_copies(g_send.at[0], early_slot, 0, at(early_shift))
-    grad_late = grad_copies(g_send.at[1], late_slot, 1, at(late_shift))
-    grad_through = grad_copies(g_recv.at[3 + last], last, 3, at(8 * first - 8 * last))
-    grad_far_through = grad_copies(g_recv.at[6], 5, 4, at(-8 * side))
+    grad_far = grad_copies(g_send.at[2], 2 + 4 * inner_end, 2, at(far_shift), HALVES)
+    grad_early = grad_copies(g_send.at[0], early_slot, 0, at(early_shift), PARTS)
+    grad_late = grad_copies(g_send.at[1], late_slot, 1, at(late_shift), PARTS)
+    grad_through = grad_copies(g_recv.at[3 + last], last, 3, at(8 * first - 8 * last), PARTS)
+    grad_far_through = grad_copies(g_recv.at[6], 5, 4, at(-8 * side), HALVES)
     pair_own, pair_early, pair_late = pair_copy(0), pair_copy(2 - core), pair_copy(1 + core)
 
-    def grad_arrived(slot, part):
-        grad_copy(g_send.at[0], slot, 0, partner, part).wait_recv()
+    def grad_arrived(slot, part, parts=PARTS):
+        grad_copy(g_send.at[0], slot, 0, partner, part, parts).wait_recv()
 
     def pair_arrived(n):
         pair_copy(n).wait_recv()
@@ -385,7 +388,8 @@
 
         @pl.when(inner_end == 0)
         def _():
-            grad_arrived(2, part)
+            if part % (PARTS // HALVES) == 0:
+                grad_arrived(2, part * HALVES // PARTS, HALVES)
             g_send[1, rows] = (
                 txt_acc[3 - core, rows]
                 + p_recv[2 - core, rows].astype(jnp.float32)
@@ -404,8 +408,8 @@
 
     @pl.when(outer_end == 1)
     def _():
-        for part in range(PARTS):
-            grad_arrived(6, part)
+        for part in range(HALVES):
+            grad_arrived(6, part, HALVES)
             grad_far_through[part].start()
 
     def go_through():
@@ -425,8 +429,32 @@
     def _():
         go_through()
 
-    inverse, full = unit_rows(img_in[...])
-    gi[...] = project_back(inverse, full, image_sum((0, 0)) * factor)
+    for slot in SLOTS[1:]:
+        gather_copy(slot).wait_send()
+        if slot not in LATE_SLOTS:
+            image_copy(slot).wait_send()
+    for copy in (pair_own, pair_early, pair_late):
+        copy.wait_send()
+    for copies in (text_partner, text_up, text_down, text_four, text_five, grad_far, grad_early):
+        for copy in copies:
+            copy.wait_send()
+
+    @pl.when(inner_end == 0)
+    def _():
+        for copy in text_far:
+            copy.wait_send()
+
+    @pl.when(outer_end == 1)
+    def _():
+        for copy in text_far_own:
+            copy.wait_send()
+
+    @pl.when(through == 1)
+    def _():
+        for copy in text_through:
+            copy.wait_send()
+
+    gi[...] = project_back(inv_img[...], gi[...], image_sum((0, 0)) * factor)
     store_img = pltpu.make_async_copy(gi, gi_hbm, out_sem.at[0])
     store_img.start()
 
@@ -445,35 +473,26 @@
 
         @pl.when(outer_end == 1)
         def _():
-            grad_arrived(5, part)
+            if part % (PARTS // HALVES) == 0:
+                grad_arrived(5, part * HALVES // PARTS, HALVES)
             txt_acc[0, rows] += g_recv[5, rows].astype(jnp.float32)
 
-        inverse, full = unit_rows(txt_in[rows, :])
-        gt[rows, :] = project_back(inverse, full, txt_acc[0, rows] * factor)
+        gt[rows, :] = project_back(inv_txt[rows, :], gt[rows, :], txt_acc[0, rows] * factor)
         store_txt(part).start()
 
-    for slot in SLOTS[1:]:
-        gather_copy(slot).wait_send()
+    for slot in LATE_SLOTS:
         image_copy(slot).wait_send()
-    for copy in (pair_own, pair_early, pair_late):
+    for copy in grad_late:
         copy.wait_send()
-    for copies in (text_partner, text_up, text_down, text_four, text_five, grad_far, grad_early, grad_late):
-        for copy in copies:
+
+    @pl.when(outer_end == 1)
+    def _():
+        for copy in grad_far_through:
             copy.wait_send()
 
-    @pl.when(inner_end == 0)
-    def _():
-        for copy in text_far:
-            copy.wait_send()
-
-    @pl.when(outer_end == 1)
-    def _():
-        for copy in text_far_own + grad_far_through:
-            copy.wait_send()
-
     @pl.when(through == 1)
     def _():
-        for copy in text_through + grad_through:
+        for copy in grad_through:
             copy.wait_send()
 
     store_img.wait()
@@ -509,6 +528,8 @@
             pltpu.VMEM((3, TXT, D), bf),
             pltpu.VMEM((IMG, D), f32),
             pltpu.VMEM((TXT, D), f32),
+            pltpu.VMEM((IMG, 1), f32),
+            pltpu.VMEM((TXT, 1), f32),
             dma((4,)), dma((1 + PARTS,)),
             dma((NI,)), dma((NI,)),
             dma((8, PARTS)), dma((9, PARTS)),

time: 68.4 us -> 68.1 us (level)
  the two profiles are of different devices: /device:TPU:2 before, /device:TPU:1 now
where the time goes in v6:
time: 68.1 us; the launch traced here: 67.8 us
  Pallas kernels  62.7 us (92%)
  local copies, waits for them, and re-layouts  3.17 us (5%)
  between operations  1.94 us (3%)
    pallas_call x1, Pallas kernels, local(): pl.pallas_call(kernel, out_shape=(jax.ShapeDtypeStruct((IMG, D), f32), ja...  62.7 us
    unnamed x6, local copies, waits for them, and re-layouts  3.17 us

profile of v6, /device:TPU:1, one launch (start us, length us, event | category | flops | bytes accessed | tf_op | source)
XLA Modules:
  0.0 67.8 jit_solution(2869696386425489932)
XLA Ops:
  1.9 0.0 copy-start
  1.9 1.0 %copy-done = bf16[128,1152]{1,0:T(8,128)(2,1)S(1)} copy-done((bf16[128,1152]{1,0:T(8,128)(2,1)S(1)}, bf16[128,1152]{1,0:T(8,128)(2,1)}, u32[]{:S(2)}) %copy-start) | copy-done | bytes 294936
  2.9 0.0 copy-start.1
  2.9 0.8 %copy-done.1 = bf16[16,1152]{1,0:T(8,128)(2,1)S(1)} copy-done((bf16[16,1152]{1,0:T(8,128)(2,1)S(1)}, bf16[16,1152]{1,0:T(8,128)(2,1)}, u32[]{:S(2)}) %copy-start.1) | copy-done | bytes 36888
  3.7 62.7 %pair_gradients.1 = (f32[16,1152]{1,0:T(8,128)S(1)}, f32[128,1152]{1,0:T(8,128)S(1)}) custom-call(f32[1]{0:T(128)S(6)} %copy.8.scale_hbm, f32[1]{0:T(128)S(6)} %copy.9.bias_hbm, bf16[16,1152]{1,0:T(8,128)(2,1)S(1)} %copy-done.1, bf16[128,1152]{1,0:T(8,128)(2,1)S(1)} %copy-done), custom_call_target="tpu_custom_call" | custom-call | tf_op jit(solution)/shard_map/pair_gradients/pallas_call | solution.py:506
  66.4 0.6 copy.10
  67.0 0.8 %copy.11 = f32[128,1152]{1,0:T(8,128)} copy(f32[128,1152]{1,0:T(8,128)S(1)} %get-tuple-element.5) | data formatting | bytes 1179648
Async XLA Ops:
  1.9 1.0 %copy-start = (bf16[128,1152]{1,0:T(8,128)(2,1)S(1)}, bf16[128,1152]{1,0:T(8,128)(2,1)}, u32[]{:S(2)}) copy-start(bf16[128,1152]{1,0:T(8,128)(2,1)} %txt_hbm.1) | copy-start | bytes 884740
  2.9 0.8 %copy-start.1 = (bf16[16,1152]{1,0:T(8,128)(2,1)S(1)}, bf16[16,1152]{1,0:T(8,128)(2,1)}, u32[]{:S(2)}) copy-start(bf16[16,1152]{1,0:T(8,128)(2,1)} %img_hbm.1) | copy-start | bytes 110596
